TPU v7x, 32 devices: a whole 2x2x4 slice. The times are simulated.
32 devices in a mesh: expert: 8 (over z, x), hidden: 4 (over y, core).
Axes of the slice: x: 2, y: 2, z: 4, core: 2. Of those that a mesh axis runs over, the one named last changes fastest.
Arguments:
- tokens: bfloat16 [16384, 512], P(('expert', 'hidden')), may hold values from -6 to 6
- lengths: int32 [32, 16], P(('expert', 'hidden')), may hold values from 1 to 256, 512 in all within a row
- task_ids: int32 [32, 16], P(('expert', 'hidden')), may hold values from 0 to 29
- routes: int32 [16384, 2], P(('expert', 'hidden')), may hold values from 0 to 7, all different within a row; in each aligned block of 512 rows (0 to 511, 512 to 1023, ...) at most 192 rows name the same one
- w_qkv: bfloat16 [512, 1536], P(('expert', 'hidden')), may hold values from -0.25 to 0.25
- w_attn_out: bfloat16 [512, 512], P(('expert', 'hidden')), may hold values from -1 to 1
- w_gate: bfloat16 [512, 240], P(('expert', 'hidden')), may hold values from -0.1875 to 0.1875
- ln1_gain: bfloat16 [512], P(('expert', 'hidden')), may hold values from 0.5 to 1.5
- ln1_bias: bfloat16 [512], P(('expert', 'hidden')), may hold values from -1 to 1
- ln2_gain: bfloat16 [512], P(('expert', 'hidden')), may hold values from 0.5 to 1.5
- ln2_bias: bfloat16 [512], P(('expert', 'hidden')), may hold values from -1 to 1
- w_in: bfloat16 [8, 512, 2048], P('expert', None, 'hidden'), may hold values from -0.25 to 0.25
- w_out: bfloat16 [8, 2048, 512], P('expert', 'hidden'), may hold values from -0.25 to 0.25
- cotangent: bfloat16 [16384, 512], P(('expert', 'hidden')), may hold values from -6 to 6
Outputs:
- layer_out: bfloat16 [16384, 512], P(('expert', 'hidden'))
- grad_tokens: float32 [16384, 512], P(('expert', 'hidden'))
- grad_w_qkv: float32 [512, 1536], P(('expert', 'hidden'))
- grad_w_attn_out: float32 [512, 512], P(('expert', 'hidden'))
- grad_w_gate: float32 [512, 240], P(('expert', 'hidden'))
- grad_ln1_gain: float32 [512], P(('expert', 'hidden'))
- grad_ln1_bias: float32 [512], P(('expert', 'hidden'))
- grad_ln2_gain: float32 [512], P(('expert', 'hidden'))
- grad_ln2_bias: float32 [512], P(('expert', 'hidden'))
- grad_w_in: float32 [8, 512, 2048], P('expert', None, 'hidden')
- grad_w_out: float32 [8, 2048, 512], P('expert', 'hidden')
Inputs may be any that keep to these rules, and one draw needn't show every extreme that they name: `lengths`: 16 sentences a pack, of 1 to 256 tokens, that fill its 512 tokens; the longest of each pack has exactly 256. `routes`: each token names 2 different experts; among the 512 tokens of one device no expert is named more than 192 times, and on some device some expert exactly 192 times.
All inputs are finite; a program needn't handle non-finite values.
Results may differ from a plain program's by a relative error of at most 0.015.
Values may be sent and summed in bfloat16 or wider, within the bound.
No kernel may reach another device: no remote copies, remote signals or barrier semaphores. Data moves between devices by JAX's collectives and lax.ppermute only.
A program may use at most 256 MiB of HBM per device.

v0:
```python
import jax
import jax.numpy as jnp
from jax import lax
from jax.sharding import PartitionSpec as P

HEADS = 8
HEAD_DIM = 64


EPS = 1e-05
BLOCK_ROWS = 512
NEG_FILL = -1e30


def layer_norm(values, gain, offset):
    middle = jnp.mean(values, axis=-1, keepdims=True)
    centred = values - middle
    spread = jnp.mean(centred * centred, axis=-1, keepdims=True)
    return centred * lax.rsqrt(spread + EPS) * gain + offset


def pack_layout(lengths, task_ids, positions):
    sentence_ends = jnp.cumsum(lengths)
    sentence = jnp.sum((positions[:, None] >= sentence_ends[None, :]).astype(jnp.int32), axis=1)
    picked = sentence[:, None] == jnp.arange(lengths.shape[0], dtype=jnp.int32)[None, :]
    task_tok = jnp.sum(jnp.where(picked, task_ids[None, :], 0), axis=1)
    return (sentence, task_tok)


def slot_layout(routes, experts):
    flat_routes = routes.reshape(-1)
    onehot = (flat_routes[:, None] == jnp.arange(experts, dtype=jnp.int32)[None, :]).astype(
        jnp.int32
    )
    earlier = jnp.cumsum(onehot, axis=0) - onehot
    slot_place = jnp.sum(earlier * onehot, axis=1)
    return (flat_routes, slot_place)


def contract_last(left, right):
    return lax.dot_general(
        left, right, (((1,), (1,)), ((), ())), preferred_element_type=jnp.float32
    )


def contract_first(left, right):
    return lax.dot_general(
        left, right, (((0,), (0,)), ((), ())), preferred_element_type=jnp.float32
    )


def body(
    tokens,
    lengths,
    task_ids,
    routes,
    w_qkv,
    w_attn_out,
    w_gate,
    ln1_gain,
    ln1_bias,
    ln2_gain,
    ln2_bias,
    w_in,
    w_out,
    cotangent,
):
    row_count, width = tokens.shape
    pair_count = routes.shape[1]
    experts = lax.axis_size("expert")
    capacity = (3 * row_count * pair_count + 2 * experts - 1) // (2 * experts)
    gathered = (
        lax.all_gather(w_qkv, ("expert", "hidden"), axis=0, tiled=True),
        lax.all_gather(w_attn_out, ("expert", "hidden"), axis=0, tiled=True),
        lax.all_gather(w_gate, ("expert", "hidden"), axis=0, tiled=True),
        lax.all_gather(ln1_gain, ("expert", "hidden"), axis=0, tiled=True),
        lax.all_gather(ln1_bias, ("expert", "hidden"), axis=0, tiled=True),
        lax.all_gather(ln2_gain, ("expert", "hidden"), axis=0, tiled=True),
        lax.all_gather(ln2_bias, ("expert", "hidden"), axis=0, tiled=True),
    )
    full_qkv, full_attn, full_gate = (gathered[0], gathered[1], gathered[2])
    gain_one = gathered[3].astype(jnp.float32)
    bias_one = gathered[4].astype(jnp.float32)
    gain_two = gathered[5].astype(jnp.float32)
    bias_two = gathered[6].astype(jnp.float32)
    positions = jnp.arange(row_count, dtype=jnp.int32)
    sentence, task_tok = pack_layout(lengths[0], task_ids[0], positions)
    inputs_full = tokens.astype(jnp.float32)
    normed_one, norm_one_back = jax.vjp(layer_norm, inputs_full, gain_one, bias_one)
    normed_low = normed_one.astype(jnp.bfloat16)
    project = jnp.dot(normed_low, full_qkv, preferred_element_type=jnp.float32).astype(jnp.bfloat16)
    queries = project[:, :width].reshape(row_count, HEADS, HEAD_DIM)
    keys_all = project[:, width : 2 * width].reshape(row_count, HEADS, HEAD_DIM)
    values_all = project[:, 2 * width :].reshape(row_count, HEADS, HEAD_DIM)
    scale = HEAD_DIM ** (-0.5)
    block = min(BLOCK_ROWS, row_count)
    block_count = row_count // block

    def scores_of():
        scores = (
            jnp.einsum("qhd,khd->hqk", queries, keys_all, preferred_element_type=jnp.float32)
            * scale
        )
        same_sentence = sentence[:, None] == sentence[None, :]
        return (jnp.where(same_sentence[None], scores, NEG_FILL), queries)

    def forward_block(block_index):
        masked, _ = scores_of()
        highest = jnp.max(masked, axis=-1, keepdims=True)
        expo = jnp.exp(masked - highest)
        totals = jnp.sum(expo, axis=-1, keepdims=True)
        probs_low = (expo / totals).astype(jnp.bfloat16)
        heads_block = jnp.einsum(
            "hqk,khd->qhd", probs_low, values_all, preferred_element_type=jnp.float32
        )
        return (heads_block.astype(jnp.bfloat16), (highest + jnp.log(totals))[..., 0])

    heads_blocks, log_totals = lax.map(forward_block, jnp.arange(block_count))
    heads = heads_blocks.reshape(row_count, width)
    attended = jnp.dot(heads, full_attn, preferred_element_type=jnp.float32)
    hidden_one = inputs_full + attended
    normed_two, norm_two_back = jax.vjp(layer_norm, hidden_one, gain_two, bias_two)
    routed_in = normed_two.astype(jnp.bfloat16)
    logits_all = jnp.dot(routed_in, full_gate, preferred_element_type=jnp.float32)
    column = task_tok[:, None] * experts + routes
    chosen = jnp.take_along_axis(logits_all, column, axis=1)
    gates = jax.nn.softmax(chosen, axis=1)
    expert_of, slot_place = slot_layout(routes, experts)
    slot_total = experts * capacity
    pair_ids = jnp.arange(row_count * pair_count, dtype=jnp.int32)
    target = expert_of * capacity + slot_place
    slot_pair = jnp.zeros((slot_total,), jnp.int32).at[target].set(pair_ids)
    slot_used = jnp.zeros((slot_total,), jnp.bool_).at[target].set(True)
    zero_low = jnp.zeros((), jnp.bfloat16)
    send_rows = jnp.where(slot_used[:, None], routed_in[slot_pair // pair_count], zero_low)
    collected = lax.all_gather(send_rows[None], "hidden", axis=0, tiled=True)
    owned = lax.all_to_all(collected, "expert", split_axis=1, concat_axis=1, tiled=True).reshape(
        -1, width
    )
    local_in = w_in[0]
    local_out = w_out[0]
    pre_act = jnp.dot(owned, local_in, preferred_element_type=jnp.float32)
    activated, gelu_back = jax.vjp(jax.nn.gelu, pre_act)
    activated = activated.astype(jnp.bfloat16)
    expert_sum = lax.psum_scatter(
        jnp.dot(activated, local_out, preferred_element_type=jnp.float32).astype(jnp.bfloat16),
        "hidden",
        scatter_dimension=0,
        tiled=True,
    )
    returned = lax.all_to_all(expert_sum, "expert", split_axis=0, concat_axis=0, tiled=True)
    paired = returned[target].reshape(row_count, pair_count, width).astype(jnp.float32)
    layer_out = hidden_one + jnp.sum(gates[:, :, None] * paired, axis=1)
    upstream = cotangent.astype(jnp.float32)
    gate_grad = jnp.sum(upstream[:, None, :] * paired, axis=2)
    pair_grad = (
        (gates[:, :, None] * upstream[:, None, :])
        .astype(jnp.bfloat16)
        .reshape(row_count * pair_count, width)
    )
    send_grads = jnp.where(slot_used[:, None], pair_grad[slot_pair], zero_low)
    grads_group = lax.all_gather(send_grads[None], "hidden", axis=0, tiled=True)
    owned_grads = lax.all_to_all(
        grads_group, "expert", split_axis=1, concat_axis=1, tiled=True
    ).reshape(-1, width)
    act_grad = contract_last(owned_grads, local_out)
    pre_grad = gelu_back(act_grad)[0].astype(jnp.bfloat16)
    grad_out_local = contract_first(activated, owned_grads)
    grad_in_local = contract_first(owned, pre_grad)
    input_sum = lax.psum_scatter(
        contract_last(pre_grad, local_in).astype(jnp.bfloat16),
        "hidden",
        scatter_dimension=0,
        tiled=True,
    )
    pair_back = lax.all_to_all(input_sum, "expert", split_axis=0, concat_axis=0, tiled=True)
    routed_grad = jnp.sum(
        pair_back[target].astype(jnp.float32).reshape(row_count, pair_count, width), axis=1
    )
    chosen_grad = gates * (gate_grad - jnp.sum(gates * gate_grad, axis=1, keepdims=True))
    gate_columns = jnp.arange(logits_all.shape[1], dtype=jnp.int32)
    logits_grad = jnp.sum(
        jnp.where(gate_columns[None, None, :] == column[:, :, None], chosen_grad[:, :, None], 0.0),
        axis=1,
    )
    logits_grad = logits_grad.astype(jnp.bfloat16)
    grad_gate = contract_first(routed_in, logits_grad)
    routed_grad = routed_grad + contract_last(logits_grad, full_gate)
    hidden_part, grad_gain_two, grad_bias_two = norm_two_back(routed_grad)
    hidden_grad = upstream + hidden_part
    attended_grad = hidden_grad.astype(jnp.bfloat16)
    grad_attn = contract_first(heads, attended_grad)
    heads_grad = (
        contract_last(attended_grad, full_attn)
        .astype(jnp.bfloat16)
        .reshape(row_count, HEADS, HEAD_DIM)
    )

    def backward_block(carry, block_index):
        key_grad, value_grad = carry
        masked, query_block = scores_of()
        probs = jnp.exp(masked - log_totals[block_index][..., None])
        prob_grad = jnp.einsum(
            "qhd,khd->hqk", heads_grad, values_all, preferred_element_type=jnp.float32
        )
        value_grad = value_grad + jnp.einsum(
            "hqk,qhd->khd",
            probs.astype(jnp.bfloat16),
            heads_grad,
            preferred_element_type=jnp.float32,
        )
        row_dot = jnp.sum(probs * prob_grad, axis=-1, keepdims=True)
        score_grad = (probs * (prob_grad - row_dot)).astype(jnp.bfloat16)
        query_grad = (
            jnp.einsum("hqk,khd->qhd", score_grad, keys_all, preferred_element_type=jnp.float32)
            * scale
        )
        key_grad = (
            key_grad
            + jnp.einsum(
                "hqk,qhd->khd", score_grad, query_block, preferred_element_type=jnp.float32
            )
            * scale
        )
        return ((key_grad, value_grad), query_grad)

    zero_heads = jnp.zeros((row_count, HEADS, HEAD_DIM), jnp.float32)
    (key_grad, value_grad), query_grad = lax.scan(
        backward_block, (zero_heads, zero_heads), jnp.arange(block_count)
    )
    qkv_grad = jnp.concatenate(
        [
            query_grad.reshape(row_count, width),
            key_grad.reshape(row_count, width),
            value_grad.reshape(row_count, width),
        ],
        axis=1,
    ).astype(jnp.bfloat16)
    grad_qkv = contract_first(normed_low, qkv_grad)
    normed_grad = contract_last(qkv_grad, full_qkv)
    input_part, grad_gain_one, grad_bias_one = norm_one_back(normed_grad)
    input_grad = hidden_grad + input_part
    shards = (
        lax.psum_scatter(grad_qkv, ("expert", "hidden"), scatter_dimension=0, tiled=True),
        lax.psum_scatter(grad_attn, ("expert", "hidden"), scatter_dimension=0, tiled=True),
        lax.psum_scatter(grad_gate, ("expert", "hidden"), scatter_dimension=0, tiled=True),
        lax.psum_scatter(grad_gain_one, ("expert", "hidden"), scatter_dimension=0, tiled=True),
        lax.psum_scatter(grad_bias_one, ("expert", "hidden"), scatter_dimension=0, tiled=True),
        lax.psum_scatter(grad_gain_two, ("expert", "hidden"), scatter_dimension=0, tiled=True),
        lax.psum_scatter(grad_bias_two, ("expert", "hidden"), scatter_dimension=0, tiled=True),
    )
    return (
        layer_out.astype(jnp.bfloat16),
        input_grad,
        shards[0],
        shards[1],
        shards[2],
        shards[3],
        shards[4],
        shards[5],
        shards[6],
        grad_in_local[None],
        grad_out_local[None],
    )


def solution(mesh):
    placed = (
        P(("expert", "hidden"), None),
        P(("expert", "hidden"), None),
        P(("expert", "hidden"), None),
        P(("expert", "hidden"), None),
        P(("expert", "hidden"), None),
        P(("expert", "hidden"), None),
        P(("expert", "hidden"), None),
        P(("expert", "hidden")),
        P(("expert", "hidden")),
        P(("expert", "hidden")),
        P(("expert", "hidden")),
        P("expert", None, "hidden"),
        P("expert", "hidden", None),
        P(("expert", "hidden"), None),
    )
    return jax.shard_map(
        body,
        mesh=mesh,
        in_specs=placed,
        out_specs=(
            P(("expert", "hidden"), None),
            P(("expert", "hidden"), None),
            P(("expert", "hidden"), None),
            P(("expert", "hidden"), None),
            P(("expert", "hidden"), None),
            P(("expert", "hidden")),
            P(("expert", "hidden")),
            P(("expert", "hidden")),
            P(("expert", "hidden")),
            P("expert", None, "hidden"),
            P("expert", "hidden", None),
        ),
        check_vma=False,
    )
```

profile of v0, /device:TPU:0, one launch (start us, length us, event | category | flops | bytes accessed | tf_op | source)
XLA Modules:
  0.0 1137.7 jit_solution(13540288396526038556)
XLA Ops:
  14.3 42.0 %all-reduce.9 = (bf16[512]{0:T(512)(128)(2,1)S(1)}, bf16[512]{0:T(512)(128)(2,1)S(1)}, bf16[512]{0:T(512)(128)(2,1)S(1)}, bf16[512]{0:T(512)(128)(2,1)S(1)}) all-reduce(bf16[512]{0:T(512)(128)(2,1)S(1)} %dynamic-update-slice.1, bf16[512]{0:T(512)(128)(2,1)S(1)} %dynamic-update-slice, ...), channel_id=1, replica_groups=mesh['expert'=8,'hidden'=4] {'expert','hidden'}, use_global_device_ids=true, to_apply=%add.1 | all-reduce | flops 2048 | bytes 8192
  66.2 3.7 mul.278
  70.0 4.3 scatter_custom_fusion.1
  74.4 4.3 scatter_custom_fusion
  78.8 41.1 %all_gather.33 = bf16[512,240]{1,0:T(8,128)(2,1)S(1)} all-gather(bf16[16,240]{1,0:T(8,128)(2,1)S(1)} %copy-done.57), channel_id=1, replica_groups=mesh['expert'=8,'hidden'=4] {'expert','hidden'}, dimensions={0}, use_global_device_ids=true | all-gather | bytes 253440 | tf_op jit(solution)/shard_map/all_gather | solution.py:75
  120.4 41.2 %all_gather.30 = bf16[512,512]{1,0:T(8,128)(2,1)} all-gather(bf16[16,512]{1,0:T(8,128)(2,1)S(1)} %copy-done.54), channel_id=1, replica_groups=mesh['expert'=8,'hidden'=4] {'expert','hidden'}, dimensions={0}, use_global_device_ids=true | all-gather | bytes 540672 | tf_op jit(solution)/shard_map/all_gather | solution.py:74
  161.6 2.5 convolution_convert_fusion.2
  178.1 8.6 gather_fusion.4
  190.0 5.4 gather_fusion.2
  195.4 5.4 gather_fusion
  200.8 3.3 bitcast_select_fusion
  204.1 44.0 %all-gather.8.cloned.1.call-done = bf16[4,1536,512]{2,1,0:T(8,128)(2,1)} async-done(((bf16[1,1536,512]{2,1,0:T(8,128)(2,1)}), bf16[4,1536,512]{2,1,0:T(8,128)(2,1)}) %all-gather.8.cloned.1.call-update) | async-done | bytes 6291472 | tf_op jit(solution)/shard_map/all_gather | solution.py:162
  248.1 10.5 copy.221
  258.6 5.7 all-to-all-start.2
  265.0 48.6 %all-gather.6.cloned.1.call-done = bf16[4,1536,512]{2,1,0:T(8,128)(2,1)} async-done(((bf16[1,1536,512]{2,1,0:T(8,128)(2,1)}), bf16[4,1536,512]{2,1,0:T(8,128)(2,1)}) %all-gather.6.cloned.1.call-update) | async-done | bytes 6291472 | tf_op jit(solution)/shard_map/all_gather | solution.py:136
  313.6 10.5 copy.215
  324.0 78.9 %all-to-all-done.2 = bf16[4,1536,512]{2,0,1:T(4,128)(2,1)} async-done(((bf16[4,1536,512]{2,0,1:T(4,128)(2,1)}), bf16[4,1536,512]{2,0,1:T(4,128)(2,1)}, u32[]{:S(2)}, u32[]{:S(2)}) %all-to-all-start.2) | async-done | bytes 6291488 | tf_op jit(solution)/shard_map/all_to_all | solution.py:163
  402.9 4.8 all-to-all-start
  407.7 4.1 copy.222
  411.8 2.6 copy-done.2
  414.5 6.4 fusion.32
  420.9 124.5 %all-to-all-done = bf16[4,1536,512]{2,0,1:T(4,128)(2,1)} async-done(((bf16[4,1536,512]{2,0,1:T(4,128)(2,1)}), bf16[4,1536,512]{2,0,1:T(4,128)(2,1)}, u32[]{:S(2)}, u32[]{:S(2)}) %all-to-all-start) | async-done | bytes 6291488 | tf_op jit(solution)/shard_map/all_to_all | solution.py:137
  545.4 7.4 copy.216
  554.1 16.4 %fusion.6 = (bf16[6144,512]{1,0:T(8,128)(2,1)}, f32[6144,512]{1,0:T(8,128)}) fusion(f32[6144,512]{1,0:T(8,128)S(1)} %copy-done.7, bf16[6144,512]{1,0:T(8,128)(2,1)} %bitcast.108, bf16[1,512,512]{2,1,0:T(8,128)(2,1)S(1)} %copy-done), kind=kOutput, calls=%fused_computation.15 | convolution fusion | flops 3284140032 | bytes 38273024 | tf_op jit(solution)/shard_map/dot_general | solution.py:142
  570.4 8.2 convolution_convert_fusion
  579.1 9.6 convolution_convert_fusion.1
  588.7 46.5 %reduce-scatter.8.cloned.1.call-done = bf16[1536,512]{1,0:T(8,128)(2,1)} async-done(((bf16[6144,512]{1,0:T(8,128)(2,1)}), bf16[1536,512]{1,0:T(8,128)(2,1)}) %reduce-scatter.8.cloned.1.call-update) | async-done | bytes 1572880 | tf_op jit(solution)/shard_map/reduce_scatter | solution.py:170
  635.2 5.5 all-to-all-start.3
  640.7 55.4 %reduce-scatter.6.cloned.1.call-done = bf16[1536,512]{1,0:T(8,128)(2,1)} async-done(((bf16[6144,512]{1,0:T(8,128)(2,1)}), bf16[1536,512]{1,0:T(8,128)(2,1)}) %reduce-scatter.6.cloned.1.call-update) | async-done | bytes 1572880 | tf_op jit(solution)/shard_map/reduce_scatter | solution.py:145
  696.2 5.5 all-to-all-start.1
  701.8 5.1 gather_fusion.3
  709.3 3.7 reduce_sum.254
  715.5 23.3 %all-to-all-done.1 = bf16[8,192,512]{2,1,0:T(8,128)(2,1)} async-done(((bf16[8,192,512]{2,1,0:T(8,128)(2,1)}), bf16[8,192,512]{2,1,0:T(8,128)(2,1)}, u32[]{:S(2)}, u32[]{:S(2)}) %all-to-all-start.1) | async-done | bytes 1572896 | tf_op jit(solution)/shard_map/all_to_all | solution.py:151
  738.8 6.8 gather_fusion.1
  745.7 3.5 reshape.381
  749.1 6.5 multiply_reduce_fusion.1
  758.2 2.9 multiply_reduce_fusion.3
  763.7 2.7 fusion.61
  770.6 5.5 multiply_reduce_fusion
  776.1 4.8 multiply_convert_fusion.1
  785.5 2.7 fusion.30
  788.3 9.2 convolution_bitcast_fusion.1
  797.5 8.4 convolution_bitcast_fusion
  807.9 4.0 fusion.66
  814.2 37.6 %all-reduce.8 = (f32[512]{0:T(512)S(1)}, f32[512]{0:T(512)S(1)}, f32[512]{0:T(512)S(1)}, f32[512]{0:T(512)S(1)}) all-reduce(f32[512]{0:T(512)S(1)} %get-tuple-element.143, f32[512]{0:T(512)S(1)} %get-tuple-element.177, f32[512]{0:T(512)S(1)} %get-tuple-element.139, ...), channel_id=7, replica_groups=mesh['expert'=8,'hidden'=4] {'expert','hidden'}, use_global_device_ids=true, to_apply=%region_32.33.clone | all-reduce | flops 2048 | bytes 16384
  859.1 34.4 %reduce-scatter.14.cloned.1.call-done = f32[16,240]{1,0:T(8,128)} async-done(((f32[512,240]{1,0:T(8,128)}), f32[16,240]{1,0:T(8,128)}) %reduce-scatter.14.cloned.1.call-update) | async-done | bytes 15376 | tf_op jit(solution)/shard_map/reduce_scatter | solution.py:246
  893.4 133.8 %reduce-scatter.12.cloned.1.call-done = f32[16,512]{1,0:T(8,128)} async-done(((f32[512,512]{1,0:T(8,128)}), f32[16,512]{1,0:T(8,128)}) %reduce-scatter.12.cloned.1.call-update) | async-done | bytes 32784 | tf_op jit(solution)/shard_map/reduce_scatter | solution.py:245
  1027.2 103.4 %reduce-scatter.10.cloned.1.call-done = f32[16,1536]{1,0:T(8,128)} async-done(((f32[512,1536]{1,0:T(8,128)}), f32[16,1536]{1,0:T(8,128)}) %reduce-scatter.10.cloned.1.call-update) | async-done | bytes 98320 | tf_op jit(solution)/shard_map/reduce_scatter | solution.py:244
  (246 shorter events, 67.3 us)
Async XLA Ops:
  7.2 545.6 %copy-start = (bf16[1,512,512]{2,1,0:T(8,128)(2,1)S(1)}, bf16[1,512,512]{2,1,0:T(8,128)(2,1)}, u32[]{:S(2)}) copy-start(bf16[1,512,512]{2,1,0:T(8,128)(2,1)} %param.25) | copy-start | bytes 1572868
  7.2 154.4 %all-gather.4.cloned.1.call-start = ((), (), s32[]{:S(2)}) async-start(), calls=%async_computation.9 | async-start | bytes 1622016 | tf_op jit(solution)/shard_map/all_gather | solution.py:73
  7.9 240.2 %all-gather.8.cloned.1.call-start = ((), (), s32[]{:S(2)}) async-start(), calls=%async_computation.12 | async-start | bytes 7864320 | tf_op jit(solution)/shard_map/all_gather | solution.py:162
  10.9 67.9 %copy-start.57 = (bf16[16,240]{1,0:T(8,128)(2,1)S(1)}, bf16[16,240]{1,0:T(8,128)(2,1)}, u32[]{:S(2)}) copy-start(bf16[16,240]{1,0:T(8,128)(2,1)} %param.20) | copy-start | bytes 23044
  56.3 105.2 %copy-start.58 = (f32[512]{0:T(512)}, f32[512]{0:T(512)S(1)}, u32[]{:S(2)}) copy-start(f32[512]{0:T(512)S(1)} %convert_element_type.104) | copy-start | bytes 6148
  56.4 105.2 %copy-start.42 = (f32[512]{0:T(512)}, f32[512]{0:T(512)S(1)}, u32[]{:S(2)}) copy-start(f32[512]{0:T(512)S(1)} %convert_element_type.103) | copy-start | bytes 6148
  56.4 119.7 %copy-start.44 = (f32[512]{0:T(512)}, f32[512]{0:T(512)S(1)}, u32[]{:S(2)}) copy-start(f32[512]{0:T(512)S(1)} %convert_element_type.111) | copy-start | bytes 6148
  61.2 59.2 %copy-start.54 = (bf16[16,512]{1,0:T(8,128)(2,1)S(1)}, bf16[16,512]{1,0:T(8,128)(2,1)}, u32[]{:S(2)}) copy-start(bf16[16,512]{1,0:T(8,128)(2,1)} %param.19) | copy-start | bytes 49156
  62.5 112.8 %copy-start.5 = (bf16[512,512]{0,1:T(8,128)(2,1)}, bf16[512,512]{0,1:T(8,128)(2,1)S(1)}, u32[]{:S(2)}) copy-start(bf16[512,512]{0,1:T(8,128)(2,1)S(1)} %copy.202) | copy-start | bytes 1572868
  63.9 109.2 %copy-start.12 = (bf16[512,512]{0,1:T(8,128)(2,1)}, bf16[512,512]{0,1:T(8,128)(2,1)S(1)}, u32[]{:S(2)}) copy-start(bf16[512,512]{0,1:T(8,128)(2,1)S(1)} %copy.218) | copy-start | bytes 1572868
  64.1 100.0 %copy-start.10 = (f32[512,512]{1,0:T(8,128)}, f32[512,512]{1,0:T(8,128)S(1)}, u32[]{:S(2)}) copy-start(f32[512,512]{1,0:T(8,128)S(1)} %copy.220) | copy-start | bytes 3145732
  70.0 8.7 copy-start.55
  119.8 57.3 %copy-start.23 = (bf16[512,240]{1,0:T(8,128)(2,1)}, bf16[512,240]{1,0:T(8,128)(2,1)S(1)}, u32[]{:S(2)}) copy-start(bf16[512,240]{1,0:T(8,128)(2,1)S(1)} %all_gather.33) | copy-start | bytes 737284
  120.0 45.4 %copy-start.38 = (f32[512]{0:T(512)}, f32[512]{0:T(512)S(1)}, u32[]{:S(2)}) copy-start(f32[512]{0:T(512)S(1)} %broadcast_multiply_fusion.3) | copy-start | bytes 6148
  120.1 46.4 %copy-start.50 = (f32[512]{0:T(512)}, f32[512]{0:T(512)S(1)}, u32[]{:S(2)}) copy-start(f32[512]{0:T(512)S(1)} %fusion.28) | copy-start | bytes 6148
  120.1 46.4 %copy-start.48 = (f32[512]{0:T(512)}, f32[512]{0:T(512)S(1)}, u32[]{:S(2)}) copy-start(f32[512]{0:T(512)S(1)} %fusion.55) | copy-start | bytes 6148
  175.8 11.0 copy-start.40
  176.0 10.7 copy-start.52
  176.7 10.0 copy-start.46
  258.6 144.3 %all-to-all-start.2 = ((bf16[4,1536,512]{2,0,1:T(4,128)(2,1)}), bf16[4,1536,512]{2,0,1:T(4,128)(2,1)}, u32[]{:S(2)}, u32[]{:S(2)}) async-start(bf16[4,1536,512]{2,0,1:T(4,128)(2,1)} %copy.221), calls=%async_computation.3 | async-start | bytes 12582912 | tf_op jit(solution)/shard_map/all_to_all | solution.py:163
  264.3 49.3 %all-gather.6.cloned.1.call-start = ((), (), s32[]{:S(2)}) async-start(), calls=%async_computation.10 | async-start | bytes 7864320 | tf_op jit(solution)/shard_map/all_gather | solution.py:136
  402.9 142.5 %all-to-all-start = ((bf16[4,1536,512]{2,0,1:T(4,128)(2,1)}), bf16[4,1536,512]{2,0,1:T(4,128)(2,1)}, u32[]{:S(2)}, u32[]{:S(2)}) async-start(bf16[4,1536,512]{2,0,1:T(4,128)(2,1)} %copy.215), calls=%async_computation | async-start | bytes 12582912 | tf_op jit(solution)/shard_map/all_to_all | solution.py:137
  407.7 227.6 %reduce-scatter.8.cloned.1.call-start = ((), (), s32[]{:S(2)}) async-start(), calls=%async_computation.13 | async-start | bytes 7864320 | tf_op jit(solution)/shard_map/reduce_scatter | solution.py:170
  545.4 8.7 copy-start.7
  578.6 117.6 %reduce-scatter.6.cloned.1.call-start = ((), (), s32[]{:S(2)}) async-start(), calls=%async_computation.11 | async-start | bytes 7864320 | tf_op jit(solution)/shard_map/reduce_scatter | solution.py:145
  588.7 113.0 %copy-start.56 = (s32[1024,1]{0,1:T(1,128)S(1)}, s32[1024,1]{0,1:T(1,128)}, u32[]{:S(2)}) copy-start(s32[1024,1]{0,1:T(1,128)} %copy-done.55) | copy-start | bytes 12292
  588.7 113.1 %copy-start.35 = (f32[8,512]{1,0:T(8,128)S(1)}, f32[8,512]{1,0:T(8,128)}, u32[]{:S(2)}) copy-start(f32[8,512]{1,0:T(8,128)} %copy-done.34) | copy-start | bytes 49156
  588.7 113.1 %copy-start.37 = (f32[8,512]{1,0:T(8,128)S(1)}, f32[8,512]{1,0:T(8,128)}, u32[]{:S(2)}) copy-start(f32[8,512]{1,0:T(8,128)} %copy-done.36) | copy-start | bytes 49156
  635.2 60.9 %all-to-all-start.3 = ((bf16[8,192,512]{2,1,0:T(8,128)(2,1)}), bf16[8,192,512]{2,1,0:T(8,128)(2,1)S(1)}, u32[]{:S(2)}, u32[]{:S(2)}) async-start(bf16[8,192,512]{2,1,0:T(8,128)(2,1)} %bitcast.121), calls=%async_computation.5 | async-start | bytes 3145728 | tf_op jit(solution)/shard_map/all_to_all | solution.py:176
  696.2 42.6 %all-to-all-start.1 = ((bf16[8,192,512]{2,1,0:T(8,128)(2,1)}), bf16[8,192,512]{2,1,0:T(8,128)(2,1)}, u32[]{:S(2)}, u32[]{:S(2)}) async-start(bf16[8,192,512]{2,1,0:T(8,128)(2,1)} %bitcast.120), calls=%async_computation.2 | async-start | bytes 3145728 | tf_op jit(solution)/shard_map/all_to_all | solution.py:151
  701.7 191.7 %reduce-scatter.14.cloned.1.call-start = ((), (), s32[]{:S(2)}) async-start(), calls=%async_computation.16 | async-start | bytes 540672 | tf_op jit(solution)/shard_map/reduce_scatter | solution.py:246
  738.8 10.4 copy-start.11
  745.6 11.4 copy-start.15
  745.6 12.5 %copy-start.4 = (f32[512,512]{0,1:T(8,128)S(1)}, f32[512,512]{0,1:T(8,128)}, u32[]{:S(2)}) copy-start(f32[512,512]{0,1:T(8,128)} %copy-done.3) | copy-start | bytes 3145732
  745.6 12.5 %copy-start.24 = (bf16[512,240]{1,0:T(8,128)(2,1)S(1)}, bf16[512,240]{1,0:T(8,128)(2,1)}, u32[]{:S(2)}) copy-start(bf16[512,240]{1,0:T(8,128)(2,1)} %copy-done.23) | copy-start | bytes 737284
  745.6 12.5 %copy-start.41 = (f32[512]{0:T(512)S(1)}, f32[512]{0:T(512)}, u32[]{:S(2)}) copy-start(f32[512]{0:T(512)} %copy-done.40) | copy-start | bytes 6148
  745.6 12.5 %copy-start.45 = (f32[512]{0:T(512)S(1)}, f32[512]{0:T(512)}, u32[]{:S(2)}) copy-start(f32[512]{0:T(512)} %copy-done.44) | copy-start | bytes 6148
  745.6 12.5 %copy-start.47 = (f32[512]{0:T(512)S(1)}, f32[512]{0:T(512)}, u32[]{:S(2)}) copy-start(f32[512]{0:T(512)} %copy-done.46) | copy-start | bytes 6148
  745.6 15.4 %copy-start.53 = (f32[512]{0:T(512)S(1)}, f32[512]{0:T(512)}, u32[]{:S(2)}) copy-start(f32[512]{0:T(512)} %copy-done.52) | copy-start | bytes 6148
  756.8 10.6 copy-start.13
  758.2 9.4 copy-start.22
  761.1 266.1 %reduce-scatter.12.cloned.1.call-start = ((), (), s32[]{:S(2)}) async-start(), calls=%async_computation.15 | async-start | bytes 1081344 | tf_op jit(solution)/shard_map/reduce_scatter | solution.py:245
  770.6 360.1 %reduce-scatter.10.cloned.1.call-start = ((), (), s32[]{:S(2)}) async-start(), calls=%async_computation.14 | async-start | bytes 3244032 | tf_op jit(solution)/shard_map/reduce_scatter | solution.py:244
  770.6 12.5 %slice-start = ((s8[8388608]{0:T(1024)(128)(4,1)}), s8[4194304]{0:T(1024)(128)(4,1)S(1)}, s32[]{:S(2)}) async-start(s8[8388608]{0:T(1024)(128)(4,1)} %bitcast.101), calls=%async_computation.17 | async-start | bytes 8388608
  785.5 12.0 %slice-start.2 = ((s8[6291456]{0:T(1024)(128)(4,1)}), s8[2097152]{0:T(1024)(128)(4,1)S(1)}, s32[]{:S(2)}) async-start(s8[6291456]{0:T(1024)(128)(4,1)} %bitcast.105), calls=%async_computation.19 | async-start | bytes 4194304
  788.3 9.2 slice-start.3
  805.9 7.8 copy-start.51
  807.9 46.2 %copy-start.9 = (f32[512,512]{0,1:T(8,128)S(1)}, f32[512,512]{0,1:T(8,128)}, u32[]{:S(2)}) copy-start(f32[512,512]{0,1:T(8,128)} %copy-done.8) | copy-start | bytes 3145732
  (28 other events, 89.3 us)
Sparse Core Ops, SparseCore 0:
  10.9 57.7 all-gather.3
  204.2 43.8 all-gather.7
  266.7 46.8 all-gather.5
  578.7 56.4 reduce-scatter.7
  637.8 58.3 reduce-scatter.5
  761.2 132.1 reduce-scatter.13
  896.3 130.8 reduce-scatter.11
  1033.2 97.4 reduce-scatter.9
where the time goes:
time: 1150 us; the launch traced here: 1140 us
  waiting for transfers between devices  694 us (60%)
  blocking collectives  162 us (14%)
  local copies, waits for them, and re-layouts  123 us (11%)
  matrix products  87.4 us (8%)
  other arithmetic  33.5 us (3%)
  starting transfers between devices  22.2 us (2%)
  between operations  15.3 us (1%)
    reduce_scatter x1, waiting for transfers between devices, body(): lax.psum_scatter(grad_attn, ('expert', 'hidden'), scatter_dimension=0, ti...  134 us
    all_to_all x1, waiting for transfers between devices, body(): lax.all_to_all(collected, 'expert', split_axis=1, concat_axis=1, tiled=True)  125 us
    reduce_scatter x1, waiting for transfers between devices, body(): lax.psum_scatter(grad_qkv, ('expert', 'hidden'), scatter_dimension=0, til...  103 us
    unnamed x2, blocking collectives  79.6 us
    all_to_all x1, waiting for transfers between devices, body(): lax.all_to_all(grads_group, 'expert', split_axis=1, concat_axis=1, tiled=...  78.9 us
    reduce_scatter x1, waiting for transfers between devices, body(): lax.psum_scatter(jnp.dot(activated, local_out, preferred_element_type=jnp...  55.4 us
    all_gather x1, waiting for transfers between devices, body(): collected = lax.all_gather(send_rows[None], 'hidden', axis=0, tiled=True)  48.6 us
    reduce_scatter x1, waiting for transfers between devices, body(): lax.psum_scatter(contract_last(pre_grad, local_in).astype(jnp.bfloat16),...  46.5 us
  transfers between devices with their start and end apart: 12, of which 10 were waited for; matrix products, arithmetic and copies ran while one was open for 12% of the time, Pallas kernels for 0%

commit v1 on v0

v1 whole, which is shorter than its diff:
```python
import functools

import jax
import jax.numpy as jnp
from jax import lax
from jax.experimental import pallas as pl
from jax.experimental.pallas import tpu as pltpu
from jax.sharding import PartitionSpec as P

HEADS = 8
HEAD_DIM = 64
EPS = 1e-05
NEG_FILL = -1e30
LANES = 128
BOTH = ("expert", "hidden")
F32 = jnp.float32
BF16 = jnp.bfloat16
VMEM_LIMIT = 56 * 1024 * 1024


def mm(left, right):
    return jnp.dot(left, right, preferred_element_type=F32)


def contract_last(left, right):
    return lax.dot_general(left, right, (((1,), (1,)), ((), ())), preferred_element_type=F32)


def contract_first(left, right):
    return lax.dot_general(left, right, (((0,), (0,)), ((), ())), preferred_element_type=F32)


def iota(shape, axis):
    return lax.broadcasted_iota(jnp.int32, shape, axis)


def iota_f(shape, axis):
    return iota(shape, axis).astype(F32)


def lane_sum(values):
    return jnp.sum(values, axis=1, keepdims=True)


def row_sum(values):
    return jnp.sum(values, axis=0, keepdims=True)


def norm_parts(values):
    middle = jnp.mean(values, axis=-1, keepdims=True)
    centred = values - middle
    spread = jnp.mean(centred * centred, axis=-1, keepdims=True)
    inverse = lax.rsqrt(spread + EPS)
    return centred * inverse, inverse


def norm_back(unit, inverse, gain, grad):
    scaled = grad * gain
    mean_one = jnp.mean(scaled, axis=-1, keepdims=True)
    mean_two = jnp.mean(scaled * unit, axis=-1, keepdims=True)
    return inverse * (scaled - mean_one - unit * mean_two)


def round_up(value, step):
    return (value + step - 1) // step * step


def call(kernel, outs, scratch, args, flops, smem=()):
    def spec(at):
        return pl.BlockSpec(memory_space=pltpu.SMEM if at in smem else pltpu.VMEM)

    touched = sum(a.size * a.dtype.itemsize for a in args) + sum(
        o.size * o.dtype.itemsize for o in jax.tree.leaves(outs)
    )
    return pl.pallas_call(
        kernel,
        out_shape=outs,
        in_specs=[spec(at) for at in range(len(args))],
        out_specs=jax.tree.map(lambda _: pl.BlockSpec(memory_space=pltpu.VMEM), outs),
        scratch_shapes=scratch,
        compiler_params=pltpu.CompilerParams(vmem_limit_bytes=VMEM_LIMIT),
        cost_estimate=pl.CostEstimate(flops=flops, bytes_accessed=touched, transcendentals=0),
    )(*args)


def shape(dims, dtype):
    return jax.ShapeDtypeStruct(dims, dtype)


def prep_kernel(experts, cap, lens_ref, tasks_ref, routes_ref, cot_ref, side_ref, rows_ref, sent_ref):
    count = routes_ref.shape[0]
    sents = lens_ref.shape[1]
    lens = lens_ref[...].astype(F32)
    tasks = tasks_ref[...].astype(F32)
    down, across = iota((sents, sents), 0), iota((sents, sents), 1)
    ends_col = lane_sum(jnp.where(across <= down, lens, 0.0))
    ends_row = row_sum(jnp.where(across == down, ends_col, 0.0))
    passed = jnp.where(iota_f((count, sents), 0) >= ends_row, 1.0, 0.0)
    sentence = lane_sum(passed)
    task = lane_sum(jnp.where(iota_f((count, sents), 1) == sentence, tasks, 0.0))
    routes = routes_ref[...].astype(F32)
    first, second = routes[:, 0:1], routes[:, 1:2]
    lane_e = iota_f((count, experts), 1)
    hot_one = jnp.where(lane_e == first, 1.0, 0.0)
    hot_two = jnp.where(lane_e == second, 1.0, 0.0)
    before = jnp.where(iota((count, count), 1) < iota((count, count), 0), 1.0, 0.0).astype(BF16)
    earlier = mm(before, (hot_one + hot_two).astype(BF16))
    target_one = first * cap + lane_sum(earlier * hot_one)
    target_two = second * cap + lane_sum(earlier * hot_two)
    lane = iota((count, LANES), 1)
    side = jnp.where(lane == 0, target_one, 0.0)
    side = jnp.where(lane == 1, target_two, side)
    side = jnp.where(lane == 2, task * experts + first, side)
    side = jnp.where(lane == 3, task * experts + second, side)
    side = jnp.where(lane == 4, sentence, side)
    side_ref[...] = side
    turned = jnp.transpose(side)
    rows_ref[...] = turned[0:8, :]
    one_row, two_row = turned[0:1, :], turned[1:2, :]
    cot = cot_ref[...]
    for e in range(experts):
        at = iota_f((cap, count), 0) + float(e * cap)
        pick = jnp.where((at == one_row) | (at == two_row), 1.0, 0.0).astype(BF16)
        sent_ref[e] = mm(pick, cot).astype(BF16)


class Groups:
    def __init__(self, devices):
        bits = devices.bit_length() - 1
        mid = (bits - 1) // 2
        self.near = [1]
        self.mid = self.masks(1, mid)
        self.far = self.masks(1 + mid, bits - 1 - mid)
        self.devices = devices

    @staticmethod
    def masks(low, width):
        return [m << low for m in range(1 << width)]

    def owners(self):
        return [[n | b | c for c in self.far] for n in (0, 1) for b in self.mid]

    def swap(self, value, mask):
        return lax.ppermute(value, BOTH, [(i, i ^ mask) for i in range(self.devices)])

    def gather(self, shard):
        far = jnp.concatenate([shard] + [self.swap(shard, m) for m in self.far[1:]], axis=0)
        mid = [far] + [self.swap(far, m) for m in self.mid[1:]]
        return mid + [self.swap(block, 1) for block in mid]


def place_blocks(owners, me, block_refs, full_ref):
    if len(block_refs) == 1:
        full_ref[...] = block_refs[0][...]
        return
    for block_ref, masks in zip(block_refs, owners):
        rows = block_ref.shape[0] // len(masks)
        for i, mask in enumerate(masks):
            at = pl.multiple_of((me ^ mask) * rows, rows)
            full_ref[pl.ds(at, rows), :] = block_ref[i * rows : (i + 1) * rows, :]


def take_blocks(owners, me, full_ref, keep_ref, send_ref):
    half = len(owners) // 2
    for n, out_ref in ((0, keep_ref), (1, send_ref)):
        for b, masks in enumerate(owners[n * half : (n + 1) * half]):
            rows = full_ref.shape[0] // (len(owners) * len(masks))
            for i, mask in enumerate(masks):
                at = pl.multiple_of((me ^ mask) * rows, rows)
                to = (b * len(masks) + i) * rows
                out_ref[to : to + rows, :] = full_ref[pl.ds(at, rows), :].astype(out_ref.dtype)


def add_kernel(parts, keep_ref, *refs):
    got, outs = refs[: len(refs) - parts], refs[len(refs) - parts :]
    rows = outs[0].shape[0]
    for i, out_ref in enumerate(outs):
        span = slice(i * rows, (i + 1) * rows)
        total = keep_ref[span, :]
        for ref in got:
            total = total + ref[span, :].astype(F32)
        out_ref[...] = total.astype(out_ref.dtype)


def add_parts(keep, got, parts):
    rows, columns = keep.shape
    outs = [shape((rows // parts, columns), F32 if i == 0 else BF16) for i in range(parts)]
    return call(functools.partial(add_kernel, parts), outs, [], [keep] + got, rows * columns * len(got))


def sum_to_owner(groups, keep, send):
    blocks = add_parts(keep, [groups.swap(send, 1)], len(groups.mid))
    got = [groups.swap(b, m) for b, m in zip(blocks[1:], groups.mid[1:])]
    blocks = add_parts(blocks[0], got, len(groups.far))
    got = [groups.swap(b, m) for b, m in zip(blocks[1:], groups.far[1:])]
    return add_parts(blocks[0], got, 1)[0]


def gain_rows(full_ref, start, gate_columns):
    tile = start + gate_columns // LANES * LANES
    lane = gate_columns % LANES
    turned = jnp.transpose(full_ref[:, tile : tile + LANES].astype(F32))
    return [turned[lane + i : lane + i + 1, :] for i in range(4)]


def forward_kernel(
    cfg, me_ref, side_ref, rows_ref, tokens_ref, *refs
):
    blocks = refs[: cfg.blocks]
    outs = refs[cfg.blocks :]
    full_ref, proj_ref, heads_ref, lse_ref, hidden_ref, gates_ref = outs[:6]
    send_refs = outs[6 : 6 + cfg.experts]
    bias_ref, routed_ref = outs[6 + cfg.experts :]
    count, width = tokens_ref.shape
    me = me_ref[0]
    place_blocks(cfg.owners, me, blocks, full_ref)
    gain_one, bias_one, gain_two, bias_two = gain_rows(full_ref, 4 * width, cfg.gate_columns)
    chunk = 128
    for c in range(count // chunk):
        span = slice(c * chunk, (c + 1) * chunk)
        unit, _ = norm_parts(tokens_ref[span, :].astype(F32))
        routed_ref[span, :] = (unit * gain_one + bias_one).astype(BF16)
        bias_ref[span, :] = jnp.where(
            side_ref[span, 4:5] == rows_ref[4:5, :], 0.0, NEG_FILL
        )
    proj_ref[...] = mm(routed_ref[...], full_ref[:, : 3 * width]).astype(BF16)
    lse_ref[...] = jnp.zeros_like(lse_ref)
    lane = iota((1, LANES), 1)
    scale = HEAD_DIM ** (-0.5)
    block = 256

    def slab(i, carry):
        off = pl.multiple_of(i * LANES, LANES)
        keys = proj_ref[:, pl.ds(width + off, LANES)]
        values = proj_ref[:, pl.ds(2 * width + off, LANES)]
        halves = []
        for half in (0, 1):
            mine = jnp.where(lane // HEAD_DIM == half, 1.0, 0.0).astype(BF16)
            halves.append((keys * mine, values * mine))
        for r in range(count // block):
            span = slice(r * block, (r + 1) * block)
            queries = proj_ref[span, pl.ds(off, LANES)]
            total = jnp.zeros((block, LANES), F32)
            logs = lse_ref[span, :]
            for half, (key_half, value_half) in enumerate(halves):
                scores = contract_last(queries, key_half) * scale + bias_ref[span, :]
                highest = jnp.max(scores, axis=1, keepdims=True)
                expo = jnp.exp(scores - highest)
                sums = lane_sum(expo)
                probs = (expo * (1.0 / sums)).astype(BF16)
                total = total + mm(probs, value_half)
                logs = jnp.where(lane == 2 * i + half, highest + jnp.log(sums), logs)
            heads_ref[span, pl.ds(off, LANES)] = total.astype(BF16)
            lse_ref[span, :] = logs
        return carry

    lax.fori_loop(0, width // LANES, slab, 0)
    for c in range(count // chunk):
        span = slice(c * chunk, (c + 1) * chunk)
        attended = mm(heads_ref[span, :], full_ref[:, 3 * width : 4 * width])
        hidden = tokens_ref[span, :].astype(F32) + attended
        hidden_ref[span, :] = hidden
        unit, _ = norm_parts(hidden)
        routed = (unit * gain_two + bias_two).astype(BF16)
        routed_ref[span, :] = routed
        logits = mm(routed, full_ref[:, 4 * width :])
        column = iota_f(logits.shape, 1)
        one = lane_sum(jnp.where(column == side_ref[span, 2:3], logits, 0.0))
        two = lane_sum(jnp.where(column == side_ref[span, 3:4], logits, 0.0))
        top = jnp.maximum(one, two)
        expo_one, expo_two = jnp.exp(one - top), jnp.exp(two - top)
        both = expo_one + expo_two
        gates_ref[span, :] = jnp.where(
            lane == 0, expo_one / both, jnp.where(lane == 1, expo_two / both, 0.0)
        )
    cap = cfg.cap
    mine = me // cfg.hidden
    routed = routed_ref[...]
    gate_lanes = round_up(cap, LANES)
    for k in range(cfg.experts):
        base = ((mine ^ k) * cap).astype(F32)
        at = iota_f((cap, count), 0) + base
        pick = (at == rows_ref[0:1, :]) | (at == rows_ref[1:2, :])
        send_refs[k][0:cap, :] = mm(jnp.where(pick, 1.0, 0.0).astype(BF16), routed).astype(BF16)
        slot = iota_f((count, gate_lanes), 1) + base
        row = row_sum(
            jnp.where(slot == side_ref[:, 0:1], gates_ref[:, 0:1], 0.0)
            + jnp.where(slot == side_ref[:, 1:2], gates_ref[:, 1:2], 0.0)
        )
        put_split(send_refs[k], cap, row)


def put_split(ref, cap, row):
    extra = ref.shape[0] - cap
    high = row.astype(BF16).astype(F32)
    down = iota((extra, row.shape[1]), 0)
    both = jnp.where(down == 0, high, jnp.where(down == 1, row - high, 0.0))
    ref[cap:, :] = jnp.zeros((extra, ref.shape[1]), BF16)
    ref[cap:, 0 : row.shape[1]] = both.astype(BF16)


def take_split(ref, cap, lanes):
    both = ref[cap:, 0:lanes].astype(F32)
    return both[0:1, :] + both[1:2, :]


def expert_kernel(cfg, me_ref, cot_ref, *refs):
    n, h = cfg.experts, cfg.hidden
    row_refs, in_refs, out_refs = refs[:n], refs[n : n + h], refs[n + h : n + 2 * h]
    outs = refs[n + 2 * h :]
    result_ref, back_refs = outs[0], outs[1 : 1 + n]
    grad_in_refs = outs[1 + n : 1 + n + h]
    grad_out_refs = outs[1 + n + h : 1 + n + 2 * h]
    rows_all, pairs_all, rows_turned, pairs_turned, result_sum, back_sum, act_all, pre_all = outs[
        1 + n + 2 * h :
    ]
    cap = cfg.cap
    total, width = rows_all.shape
    mine = me_ref[0] // h
    gate_lanes = round_up(cap, LANES)
    eye = iota((cap, gate_lanes), 0) == iota((cap, gate_lanes), 1)
    for k in range(n):
        span = slice(k * cap, (k + 1) * cap)
        rows_all[span, :] = row_refs[k][0:cap, :]
        gate = lane_sum(jnp.where(eye, take_split(row_refs[k], cap, gate_lanes), 0.0))
        pairs_all[span, :] = (gate * cot_ref[mine ^ k].astype(F32)).astype(BF16)
    rows_turned[...] = jnp.transpose(rows_all[...])
    pairs_turned[...] = jnp.transpose(pairs_all[...])
    tile = 256
    root = 0.7978845608028654
    cubic = 0.044715
    for b in range(h):
        w_in, w_out = in_refs[b], out_refs[b]

        def step(m, carry):
            span = pl.ds(pl.multiple_of(m * tile, tile), tile)
            pre = mm(rows_all[span, :], w_in[...])
            square = pre * pre
            bent = jnp.tanh(pre * (root + (root * cubic) * square))
            upper = 0.5 + 0.5 * bent
            act = pre * upper
            slope = upper + act * (1.0 - upper) * (2.0 * root + (6.0 * root * cubic) * square)
            act_low = act.astype(BF16)
            act_all[span, :] = act_low
            act_grad = contract_last(pairs_all[span, :], w_out[...])
            pre_grad = (act_grad * slope).astype(BF16)
            pre_all[span, :] = pre_grad
            result = mm(act_low, w_out[...])
            back = contract_last(pre_grad, w_in[...])
            if b == 0:
                result_sum[span, :] = result
                back_sum[span, :] = back
            else:
                result_sum[span, :] += result
                back_sum[span, :] += back
            return carry

        lax.fori_loop(0, total // tile, step, 0)
        grad_in_refs[b][...] = mm(rows_turned[...], pre_all[...]).astype(grad_in_refs[b].dtype)
        grad_out_refs[b][...] = mm(pairs_turned[...], act_all[...]).astype(grad_out_refs[b].dtype)
    for k in range(n):
        span = slice(k * cap, (k + 1) * cap)
        result = result_sum[span, :].astype(BF16)
        result_ref[mine ^ k] = result
        back_refs[k][0:cap, :] = back_sum[span, :].astype(BF16)
        dots = lane_sum(cot_ref[mine ^ k].astype(F32) * result.astype(F32))
        put_split(back_refs[k], cap, row_sum(jnp.where(eye, dots, 0.0)))


def turn_add_kernel(own_in, own_out, got_in, got_out, more_in, more_out, sum_in, sum_out):
    sum_in[...] = own_in[...] + got_in[...].astype(F32) + more_in[...].astype(F32)
    whole = own_out[...] + got_out[...].astype(F32) + more_out[...].astype(F32)
    sum_out[...] = jnp.transpose(whole)


def backward_kernel(cfg, me_ref, side_ref, hidden_ref, gates_ref, cot_ref, heads_ref, full_ref, *refs):
    n, cap = cfg.experts, cfg.cap
    back_refs = refs[:n]
    hidden_grad_ref, heads_grad_ref = refs[n : n + 2]
    dense = refs[n + 2 : len(refs) - 4]
    routed_sum, dense_ref, routed_ref, logits_ref = refs[len(refs) - 4 :]
    count, width = hidden_ref.shape
    me = me_ref[0]
    mine = me // cfg.hidden
    gain_one, bias_one, gain_two, bias_two = gain_rows(full_ref, 4 * width, cfg.gate_columns)
    gate_lanes = round_up(cap, LANES)
    one, two = side_ref[:, 0:1], side_ref[:, 1:2]
    dot_one = jnp.zeros((count, 1), F32)
    dot_two = jnp.zeros((count, 1), F32)
    for k in range(n):
        base = ((mine ^ k) * cap).astype(F32)
        slot = iota_f((count, cap), 1) + base
        pick = jnp.where((slot == one) | (slot == two), 1.0, 0.0).astype(BF16)
        part = mm(pick, back_refs[k][0:cap, :])
        if k == 0:
            routed_sum[...] = part
        else:
            routed_sum[...] += part
        lane_at = iota_f((count, gate_lanes), 1)
        slot = jnp.where(lane_at < cap, lane_at + base, -1.0)
        dots = take_split(back_refs[k], cap, gate_lanes)
        dot_one = dot_one + lane_sum(jnp.where(slot == one, dots, 0.0))
        dot_two = dot_two + lane_sum(jnp.where(slot == two, dots, 0.0))
    gate_one, gate_two = gates_ref[:, 0:1], gates_ref[:, 1:2]
    shared = gate_one * dot_one + gate_two * dot_two
    chosen_one = gate_one * (dot_one - shared)
    chosen_two = gate_two * (dot_two - shared)
    gate_full = full_ref[:, 4 * width :]
    chunk = 128
    gain_sum = jnp.zeros((1, width), F32)
    bias_sum = jnp.zeros((1, width), F32)
    for c in range(count // chunk):
        span = slice(c * chunk, (c + 1) * chunk)
        column = iota_f((chunk, cfg.gate_lanes), 1)
        logits = jnp.where(column == side_ref[span, 2:3], chosen_one[span], 0.0) + jnp.where(
            column == side_ref[span, 3:4], chosen_two[span], 0.0
        )
        logits = logits.astype(BF16)
        logits_ref[span, :] = logits
        routed_grad = routed_sum[span, :] + contract_last(logits, gate_full)
        unit, inverse = norm_parts(hidden_ref[span, :])
        routed_ref[span, :] = (unit * gain_two + bias_two).astype(BF16)
        gain_sum = gain_sum + row_sum(routed_grad * unit)
        bias_sum = bias_sum + row_sum(routed_grad)
        hidden_grad = cot_ref[span, :].astype(F32) + norm_back(unit, inverse, gain_two, routed_grad)
        hidden_grad_ref[span, :] = hidden_grad
        low = hidden_grad.astype(BF16)
        routed_sum[span, :] = hidden_grad
        heads_grad_ref[span, :] = contract_last(low, full_ref[:, 3 * width : 4 * width]).astype(BF16)
    dense_ref[:, 0:width] = contract_first(heads_ref[...], routed_sum[...].astype(BF16))
    dense_ref[:, width:] = contract_first(routed_ref[...], logits_ref[...])
    tile = width + cfg.gate_columns // LANES * LANES
    lane = cfg.gate_columns % LANES
    dense_ref[:, tile : tile + LANES] += rows_to_lanes(gain_sum, bias_sum, lane + 2)
    put_dense(cfg, me, dense_ref, dense)


def rows_to_lanes(first, second, lane):
    down = iota((LANES, first.shape[1]), 0)
    return jnp.transpose(jnp.where(down == lane, first, jnp.where(down == lane + 1, second, 0.0)))


def put_dense(cfg, me, dense_ref, outs):
    if len(outs) == 1:
        outs[0][...] = dense_ref[...]
    else:
        take_blocks(cfg.owners, me, dense_ref, *outs)


def attention_back_kernel(
    cfg, me_ref, side_ref, rows_ref, tokens_ref, proj_ref, lse_ref, heads_grad_ref, hidden_grad_ref, full_ref, *refs
):
    grad_ref = refs[0]
    dense = refs[1 : len(refs) - 4]
    bias_ref, low_ref, qkv_ref, dense_ref = refs[len(refs) - 4 :]
    count, width = tokens_ref.shape
    me = me_ref[0]
    gain_one, bias_one, gain_two, bias_two = gain_rows(full_ref, 4 * width, cfg.gate_columns)
    chunk = 128
    for c in range(count // chunk):
        span = slice(c * chunk, (c + 1) * chunk)
        unit, _ = norm_parts(tokens_ref[span, :].astype(F32))
        low_ref[span, :] = (unit * gain_one + bias_one).astype(BF16)
        bias_ref[span, :] = jnp.where(
            side_ref[span, 4:5] == rows_ref[4:5, :], 0.0, NEG_FILL
        )
    lane = iota((1, LANES), 1)
    scale = HEAD_DIM ** (-0.5)

    def slab(i, carry):
        off = pl.multiple_of(i * LANES, LANES)
        queries = proj_ref[:, pl.ds(off, LANES)]
        keys = proj_ref[:, pl.ds(width + off, LANES)]
        values = proj_ref[:, pl.ds(2 * width + off, LANES)]
        grads = heads_grad_ref[:, pl.ds(off, LANES)]
        query_grad = jnp.zeros((count, LANES), F32)
        key_grad = jnp.zeros((count, LANES), F32)
        value_grad = jnp.zeros((count, LANES), F32)
        for half in (0, 1):
            mine = jnp.where(lane // HEAD_DIM == half, 1.0, 0.0).astype(BF16)
            query_half, key_half, grads_half = queries * mine, keys * mine, grads * mine
            logs = lane_sum(jnp.where(lane == 2 * i + half, lse_ref[...], 0.0))
            probs = jnp.exp(contract_last(queries, key_half) * scale + bias_ref[...] - logs)
            prob_grad = contract_last(grads_half, values)
            row_dot = lane_sum(probs * prob_grad)
            score_grad = (probs * (prob_grad - row_dot)).astype(BF16)
            value_grad = value_grad + contract_first(probs.astype(BF16), grads_half)
            query_grad = query_grad + mm(score_grad, key_half)
            key_grad = key_grad + contract_first(score_grad, query_half)
        qkv_ref[:, pl.ds(off, LANES)] = (query_grad * scale).astype(BF16)
        qkv_ref[:, pl.ds(width + off, LANES)] = (key_grad * scale).astype(BF16)
        qkv_ref[:, pl.ds(2 * width + off, LANES)] = value_grad.astype(BF16)
        return carry

    lax.fori_loop(0, width // LANES, slab, 0)
    dense_ref[:, : 3 * width] = contract_first(low_ref[...], qkv_ref[...])
    gain_sum = jnp.zeros((1, width), F32)
    bias_sum = jnp.zeros((1, width), F32)
    for c in range(count // chunk):
        span = slice(c * chunk, (c + 1) * chunk)
        normed_grad = contract_last(qkv_ref[span, :], full_ref[:, : 3 * width])
        unit, inverse = norm_parts(tokens_ref[span, :].astype(F32))
        gain_sum = gain_sum + row_sum(normed_grad * unit)
        bias_sum = bias_sum + row_sum(normed_grad)
        grad_ref[span, :] = hidden_grad_ref[span, :] + norm_back(unit, inverse, gain_one, normed_grad)
    dense_ref[:, 3 * width :] = rows_to_lanes(gain_sum, bias_sum, 0)
    put_dense(cfg, me, dense_ref, dense)


def output_kernel(cfg, side_ref, hidden_ref, gates_ref, result_ref, out_ref):
    cap = cfg.cap
    count = hidden_ref.shape[0]
    total_one = jnp.zeros(hidden_ref.shape, F32)
    total_two = jnp.zeros(hidden_ref.shape, F32)
    for e in range(cfg.experts):
        slot = iota_f((count, cap), 1) + float(e * cap)
        pick_one = jnp.where(slot == side_ref[:, 0:1], 1.0, 0.0).astype(BF16)
        pick_two = jnp.where(slot == side_ref[:, 1:2], 1.0, 0.0).astype(BF16)
        total_one = total_one + mm(pick_one, result_ref[e])
        total_two = total_two + mm(pick_two, result_ref[e])
    mixed = gates_ref[:, 0:1] * total_one + gates_ref[:, 1:2] * total_two
    out_ref[...] = (hidden_ref[...] + mixed).astype(BF16)


class Config:
    pass


def swap_hidden(value, mask):
    size = lax.axis_size("hidden")
    return lax.ppermute(value, "hidden", [(i, i ^ mask) for i in range(size)])


def swap_expert(value, mask):
    size = lax.axis_size("expert")
    return lax.ppermute(value, "expert", [(i, i ^ mask) for i in range(size)])


def gather_hidden(own):
    size = lax.axis_size("hidden")
    blocks = {0: own}
    bit = size // 2
    while bit:
        blocks.update({at ^ bit: swap_hidden(block, bit) for at, block in list(blocks.items())})
        bit //= 2
    return [blocks[i] for i in range(size)]


def sum_hidden(blocks):
    size = len(blocks)
    held = {i: [b] for i, b in enumerate(blocks)}
    bit = 1
    while bit < size:
        low = {i: v for i, v in held.items() if not i & bit}
        for i in low:
            terms = held[i ^ bit]
            value = terms[0] if len(terms) == 1 else sum(t.astype(F32) for t in terms).astype(BF16)
            low[i] = low[i] + [swap_hidden(value, bit)]
        held = low
        bit *= 2
    return held[0]


def body(
    tokens,
    lengths,
    task_ids,
    routes,
    w_qkv,
    w_attn_out,
    w_gate,
    ln1_gain,
    ln1_bias,
    ln2_gain,
    ln2_bias,
    w_in,
    w_out,
    cotangent,
):
    count, width = tokens.shape
    cfg = Config()
    cfg.experts = lax.axis_size("expert")
    cfg.hidden = lax.axis_size("hidden")
    experts, hidden = cfg.experts, cfg.hidden
    cfg.cap = cap = (3 * count * routes.shape[1] + 2 * experts - 1) // (2 * experts)
    cfg.gate_columns = w_gate.shape[1]
    cfg.gate_lanes = round_up(cfg.gate_columns + 4, LANES)
    devices = experts * hidden
    groups = Groups(devices)
    shard_rows = w_qkv.shape[0]
    staged = shard_rows % 16 == 0
    cfg.owners = groups.owners()
    me = (lax.axis_index("expert") * hidden + lax.axis_index("hidden")).astype(jnp.int32)[None]
    extra = 16
    units = w_in.shape[2]
    slots = experts * cap
    wide = 4 * width + cfg.gate_lanes
    one_dot = 2 * count * width * width

    packed = jnp.concatenate(
        [w_qkv, w_attn_out, w_gate]
        + [v[:, None] for v in (ln1_gain, ln1_bias, ln2_gain, ln2_bias)]
        + [jnp.zeros((shard_rows, cfg.gate_lanes - cfg.gate_columns - 4), BF16)],
        axis=1,
    )
    if staged:
        dense_blocks = groups.gather(packed)
    else:
        dense_blocks = [lax.all_gather(packed, BOTH, axis=0, tiled=True)]
    cfg.blocks = len(dense_blocks)

    side, rows, sent_cot = call(
        functools.partial(prep_kernel, experts, cap),
        [
            shape((count, LANES), F32),
            shape((8, count), F32),
            shape((experts, cap, width), BF16),
        ],
        [],
        [lengths, task_ids, routes, cotangent],
        3 * one_dot,
    )
    owned_cot = lax.all_to_all(sent_cot, "expert", split_axis=0, concat_axis=0, tiled=True)
    w_in_blocks = gather_hidden(w_in[0])
    w_out_blocks = gather_hidden(w_out[0])

    outs = call(
        functools.partial(forward_kernel, cfg),
        [
            shape((width, wide), BF16),
            shape((count, 3 * width), BF16),
            shape((count, width), BF16),
            shape((count, LANES), F32),
            shape((count, width), F32),
            shape((count, LANES), F32),
        ]
        + [shape((cap + extra, width), BF16)] * experts,
        [pltpu.VMEM((count, count), F32), pltpu.VMEM((count, width), BF16)],
        [me, side, rows, tokens] + dense_blocks,
        12 * one_dot,
        smem=(0,),
    )
    full, proj, heads, lse, hidden_one, gates = outs[:6]
    send_rows = outs[6:]
    owned_rows = [send_rows[0]] + [swap_expert(send_rows[k], k) for k in range(1, experts)]

    outs = call(
        functools.partial(expert_kernel, cfg),
        [shape((experts, cap, width), BF16)]
        + [shape((cap + extra, width), BF16)] * experts
        + [shape((width, units), F32 if i == 0 else BF16) for i in range(hidden)]
        + [shape((width, units), F32 if i == 0 else BF16) for i in range(hidden)],
        [
            pltpu.VMEM((slots, width), BF16),
            pltpu.VMEM((slots, width), BF16),
            pltpu.VMEM((width, slots), BF16),
            pltpu.VMEM((width, slots), BF16),
            pltpu.VMEM((slots, width), F32),
            pltpu.VMEM((slots, width), F32),
            pltpu.VMEM((slots, units), BF16),
            pltpu.VMEM((slots, units), BF16),
        ],
        [me, owned_cot] + owned_rows + w_in_blocks + w_out_blocks,
        12 * slots * width * units * hidden,
        smem=(0,),
    )
    result, back_rows = outs[0], outs[1 : 1 + experts]
    grad_in_blocks = outs[1 + experts : 1 + experts + hidden]
    grad_out_blocks = outs[1 + experts + hidden :]
    back = [back_rows[0]] + [swap_expert(back_rows[k], k) for k in range(1, experts)]
    returned = lax.all_to_all(result, "expert", split_axis=0, concat_axis=0, tiled=True)

    in_terms = sum_hidden(grad_in_blocks)
    out_terms = sum_hidden(grad_out_blocks)
    if len(in_terms) == 3:
        grad_in, grad_out = call(
            turn_add_kernel,
            [shape((width, units), F32), shape((units, width), F32)],
            [],
            [in_terms[0], out_terms[0], in_terms[1], out_terms[1], in_terms[2], out_terms[2]],
            4 * width * units,
        )
    else:
        grad_in = sum(t.astype(F32) for t in in_terms)
        grad_out = sum(t.astype(F32) for t in out_terms).T

    def dense_shapes(columns):
        if staged:
            half = width // 2
            return [shape((half, columns), F32), shape((half, columns), BF16)]
        return [shape((width, columns), F32)]

    def dense_sum(parts):
        if staged:
            return sum_to_owner(groups, *parts)
        return lax.psum_scatter(parts[0], BOTH, scatter_dimension=0, tiled=True)

    columns_one = width + cfg.gate_lanes
    outs = call(
        functools.partial(backward_kernel, cfg),
        [shape((count, width), F32), shape((count, width), BF16)] + dense_shapes(columns_one),
        [
            pltpu.VMEM((count, width), F32),
            pltpu.VMEM((width, columns_one), F32),
            pltpu.VMEM((count, width), BF16),
            pltpu.VMEM((count, cfg.gate_lanes), BF16),
        ],
        [me, side, hidden_one, gates, cotangent, heads, full] + back,
        7 * one_dot,
        smem=(0,),
    )
    hidden_grad, heads_grad = outs[:2]
    dense_one = dense_sum(outs[2:])

    columns_two = 3 * width + LANES
    outs = call(
        functools.partial(attention_back_kernel, cfg),
        [shape((count, width), F32)] + dense_shapes(columns_two),
        [
            pltpu.VMEM((count, count), F32),
            pltpu.VMEM((count, width), BF16),
            pltpu.VMEM((count, 3 * width), BF16),
            pltpu.VMEM((width, columns_two), F32),
        ],
        [me, side, rows, tokens, proj, lse, heads_grad, hidden_grad, full],
        12 * one_dot,
        smem=(0,),
    )
    grad_tokens = outs[0]
    dense_two = dense_sum(outs[1:])

    layer_out = call(
        functools.partial(output_kernel, cfg),
        shape((count, width), BF16),
        [],
        [side, hidden_one, gates, returned],
        6 * one_dot,
    )
    first = width + cfg.gate_columns
    return (
        layer_out,
        grad_tokens,
        dense_two[:, : 3 * width],
        dense_one[:, :width],
        dense_one[:, width:first],
        dense_two[:, 3 * width],
        dense_two[:, 3 * width + 1],
        dense_one[:, first + 2],
        dense_one[:, first + 3],
        grad_in[None],
        grad_out[None],
    )


def solution(mesh):
    split = P(BOTH, None)
    vector = P(BOTH)
    placed = (split,) * 7 + (vector,) * 4 + (P("expert", None, "hidden"), P("expert", "hidden", None), split)
    return jax.shard_map(
        body,
        mesh=mesh,
        in_specs=placed,
        out_specs=(split,) * 5
        + (vector,) * 4
        + (P("expert", None, "hidden"), P("expert", "hidden", None)),
        check_vma=False,
    )
```

time: 1150 us -> 364 us (0.32)
  waiting for transfers between devices: 694 us -> 151 us
  blocking collectives: 162 us -> 0 us
  Pallas kernels: 0 us -> 105 us
  local copies, waits for them, and re-layouts: 123 us -> 18.5 us
  matrix products: 87.4 us -> 0 us
  starting transfers between devices: 22.2 us -> 87.2 us
  other arithmetic: 33.5 us -> 0.29 us
  between operations: 15.3 us -> 1.16 us
    reduce_scatter x5 -> x0, waiting for transfers between devices: 374 us -> none  [the longest x1 134 us: body(): lax.psum_scatter(grad_attn, ('expert', 'hidden'), scatter_dimension=0, ti...]
    all_to_all x4 -> x2, waiting for transfers between devices: 227 us -> 0.01 us  [the longest x1 0.01 us: body(): lax.all_to_all(sent_cot, 'expert', split_axis=0, concat_axis=0, tiled=True)]
    ppermute x0 -> x50, waiting for transfers between devices: none -> 151 us  [the longest x14 74.5 us: swap_expert(): return lax.ppermute(value, 'expert', [(i, i ^ mask) for i in range(size)])]
    pallas_call x0 -> x13, Pallas kernels: none -> 105 us  [call(): pl.pallas_call(kernel, out_shape=outs, in_specs=[spec(at) for at in range...]
    all_gather x3 -> x0, waiting for transfers between devices: 92.6 us -> none  [the longest x1 48.6 us: body(): collected = lax.all_gather(send_rows[None], 'hidden', axis=0, tiled=True)]
    dot_general x21 -> x0, matrix products: 87.4 us -> none  [the longest x5 24 us: contract_first(): lax.dot_general(left, right, (((0,), (0,)), ((), ())), preferred_element_...]
    all_gather x2 -> x0, blocking collectives: 82.3 us -> none  [the longest x1 41.2 us: body(): lax.all_gather(w_attn_out, ('expert', 'hidden'), axis=0, tiled=True)]
    unnamed x2 -> x0, blocking collectives: 79.6 us -> none
  transfers between devices with their start and end apart: 12 -> 52, of which waited for: 10 -> 20; matrix products, arithmetic and copies ran while one was open for 12% -> 2% of each run, Pallas kernels for 0% -> 16%
where the time goes in v1:
time: 364 us; the launch traced here: 363 us
  waiting for transfers between devices  151 us (41%)
  Pallas kernels  105 us (29%)
  starting transfers between devices  87.2 us (24%)
  local copies, waits for them, and re-layouts  18.5 us (5%)
    pallas_call x13, Pallas kernels, call(): pl.pallas_call(kernel, out_shape=outs, in_specs=[spec(at) for at in range...  105 us
    ppermute x14, waiting for transfers between devices, swap_expert(): return lax.ppermute(value, 'expert', [(i, i ^ mask) for i in range(size)])  74.5 us
    ppermute x24, waiting for transfers between devices, swap(): lax.ppermute(value, BOTH, [(i, i ^ mask) for i in range(self.devices)])  66.1 us
    ppermute x14, starting transfers between devices, swap_expert(): return lax.ppermute(value, 'expert', [(i, i ^ mask) for i in range(size)])  31.3 us
    ppermute x24, starting transfers between devices, swap(): lax.ppermute(value, BOTH, [(i, i ^ mask) for i in range(self.devices)])  30.7 us
    all_to_all x1, starting transfers between devices, body(): lax.all_to_all(result, 'expert', split_axis=0, concat_axis=0, tiled=True)  11.5 us
    unnamed x133, local copies, waits for them, and re-layouts  10.9 us
    ppermute x12, waiting for transfers between devices, swap_hidden(): return lax.ppermute(value, 'hidden', [(i, i ^ mask) for i in range(size)])  10.4 us
  transfers between devices with their start and end apart: 52, of which 20 were waited for; matrix products, arithmetic and copies ran while one was open for 2% of the time, Pallas kernels for 16%

profile of v1, /device:TPU:0, one launch (start us, length us, event | category | flops | bytes accessed | tf_op | source)
XLA Modules:
  0.0 362.9 jit_solution(5284362557302914358)
XLA Ops:
  0.6 1.5 copy.30.routes_ref
  2.2 4.8 %shard_map.221 = (f32[512,128]{1,0:T(8,128)}, f32[8,512]{1,0:T(8,128)}, bf16[8,192,512]{2,1,0:T(8,128)(2,1)}) custom-call(s32[1,16]{1,0:T(1,128)} %lens_ref.1, s32[1,16]{1,0:T(1,128)} %tasks_ref.1, s32[512,2]{1,0:T(8,128)} %copy.30.routes_ref, bf16[512,512]{1,0:T(8,128)(2,1)} %cot_ref.3), custom_call_target="tpu_custom_call" | custom-call | flops 805306368 | bytes 2379904 | tf_op jit(solution)/shard_map/pallas_call | solution.py:75
  7.1 7.4 %all-to-all-start = ((bf16[8,192,512]{2,1,0:T(8,128)(2,1)}), bf16[8,192,512]{2,1,0:T(8,128)(2,1)S(1)}, u32[]{:S(2)}, u32[]{:S(2)}) async-start(bf16[8,192,512]{2,1,0:T(8,128)(2,1)} %get-tuple-element.74), calls=%async_computation | async-start | bytes 3145728 | tf_op jit(solution)/shard_map/all_to_all | solution.py:623
  15.0 3.8 %collective-permute-start.2 = (bf16[16,2304]{1,0:T(8,128)(2,1)S(1)}, bf16[16,2304]{1,0:T(8,128)(2,1)S(1)}, u32[]{:S(2)}, u32[]{:S(2)}) collective-permute-start(bf16[16,2304]{1,0:T(8,128)(2,1)S(1)} %concatenate.6), channel_id=1, source_target_pairs={{0,24},{1,25},{2,26},{3,27},{4,28},{5,29},{6,30},{7,31},{8,16},{9,... | collective-permute-start | bytes 221192 | tf_op jit(solution)/shard_map/ppermute | solution.py:144
  19.5 27.6 %collective-permute-done.2 = bf16[16,2304]{1,0:T(8,128)(2,1)S(1)} collective-permute-done((bf16[16,2304]{1,0:T(8,128)(2,1)S(1)}, bf16[16,2304]{1,0:T(8,128)(2,1)S(1)}, u32[]{:S(2)}, u32[]{:S(2)}) %collective-permute-start.2) | collective-permute-done | bytes 73760 | tf_op jit(solution)/shard_map/ppermute | solution.py:144
  47.1 10.7 %collective-permute-done.1 = bf16[16,2304]{1,0:T(8,128)(2,1)S(1)} collective-permute-done((bf16[16,2304]{1,0:T(8,128)(2,1)S(1)}, bf16[16,2304]{1,0:T(8,128)(2,1)S(1)}, u32[]{:S(2)}, u32[]{:S(2)}) %collective-permute-start.1) | collective-permute-done | bytes 73760 | tf_op jit(solution)/shard_map/ppermute | solution.py:144
  57.9 2.4 collective-permute-start.5
  61.4 7.4 %collective-permute-done.5.refs_3_ = bf16[64,2304]{1,0:T(8,128)(2,1)S(1)} collective-permute-done((bf16[64,2304]{1,0:T(8,128)(2,1)S(1)}, bf16[64,2304]{1,0:T(8,128)(2,1)S(1)}, u32[]{:S(2)}, u32[]{:S(2)}) %collective-permute-start.5) | collective-permute-done | bytes 294944 | tf_op jit(solution)/shard_map/ppermute | solution.py:144
  68.8 3.7 %collective-permute-done.4.refs_2_ = bf16[64,2304]{1,0:T(8,128)(2,1)S(1)} collective-permute-done((bf16[64,2304]{1,0:T(8,128)(2,1)S(1)}, bf16[64,2304]{1,0:T(8,128)(2,1)S(1)}, u32[]{:S(2)}, u32[]{:S(2)}) %collective-permute-start.4) | collective-permute-done | bytes 294944 | tf_op jit(solution)/shard_map/ppermute | solution.py:144
  76.0 15.9 %shard_map.222 = (bf16[512,2304]{1,0:T(8,128)(2,1)}, bf16[512,1536]{1,0:T(8,128)(2,1)}, bf16[512,512]{1,0:T(8,128)(2,1)}, f32[512,128]{1,0:T(8,128)}, f32[512,51...) custom-call(s32[1]{0:T(128)} %bitcast.me_ref, ...), custom_call_target="tpu_custom_call" | custom-call | flops 3221225472 | bytes 10895364 | tf_op jit(solution)/shard_map/pallas_call | solution.py:75
  91.9 1.8 collective-permute-start.10
  93.9 4.5 %collective-permute-done.21.refs_14_ = bf16[512,512]{1,0:T(8,128)(2,1)} collective-permute-done((bf16[512,512]{1,0:T(8,128)(2,1)S(1)}, bf16[512,512]{1,0:T(8,128)(2,1)}, u32[]{:S(2)}, u32[]{:S(2)}) %collective-permute-start.21) | collective-permute-done | bytes 524320 | tf_op jit(solution)/shard_map/ppermute | solution.py:531
  99.1 2.4 collective-permute-start.12
  103.0 8.2 %collective-permute-done.11.refs_2_ = bf16[208,512]{1,0:T(8,128)(2,1)S(1)} collective-permute-done((bf16[208,512]{1,0:T(8,128)(2,1)}, bf16[208,512]{1,0:T(8,128)(2,1)S(1)}, u32[]{:S(2)}, u32[]{:S(2)}) %collective-permute-start.11) | collective-permute-done | bytes 213024 | tf_op jit(solution)/shard_map/ppermute | solution.py:536
  111.2 2.1 collective-permute-start.14
  113.3 3.3 collective-permute-done.12.refs_3_
  116.6 2.7 collective-permute-start.15
  120.1 15.8 %collective-permute-done.14.refs_5_ = bf16[208,512]{1,0:T(8,128)(2,1)S(1)} collective-permute-done((bf16[208,512]{1,0:T(8,128)(2,1)}, bf16[208,512]{1,0:T(8,128)(2,1)S(1)}, u32[]{:S(2)}, u32[]{:S(2)}) %collective-permute-start.14) | collective-permute-done | bytes 213024 | tf_op jit(solution)/shard_map/ppermute | solution.py:536
  138.6 35.9 %shard_map.223 = (bf16[8,192,512]{2,1,0:T(8,128)(2,1)}, bf16[208,512]{1,0:T(8,128)(2,1)}, bf16[208,512]{1,0:T(8,128)(2,1)}, bf16[208,512]{1,0:T(8,128)(2,1)}, bf...) custom-call(s32[1]{0:T(128)} %bitcast.me_ref, ...), custom_call_target="tpu_custom_call" | custom-call | flops 19327352832 | bytes 15990788 | tf_op jit(solution)/shard_map/pallas_call | solution.py:75
  174.6 11.5 %all-to-all-start.1 = ((bf16[8,192,512]{2,1,0:T(8,128)(2,1)}), bf16[8,192,512]{2,1,0:T(8,128)(2,1)S(1)}, u32[]{:S(2)}, u32[]{:S(2)}) async-start(bf16[8,192,512]{2,1,0:T(8,128)(2,1)} %get-tuple-element.83), calls=%async_computation.1 | async-start | bytes 3145728 | tf_op jit(solution)/shard_map/all_to_all | solution.py:671
  186.2 2.0 collective-permute-start.23
  189.7 2.8 collective-permute-start.26
  194.0 10.8 %collective-permute-done.23.refs_1_ = bf16[208,512]{1,0:T(8,128)(2,1)S(1)} collective-permute-done((bf16[208,512]{1,0:T(8,128)(2,1)S(1)}, bf16[208,512]{1,0:T(8,128)(2,1)S(1)}, u32[]{:S(2)}, u32[]{:S(2)}) %collective-permute-start.23) | collective-permute-done | bytes 213024 | tf_op jit(solution)/shard_map/ppermute | solution.py:536
  204.8 7.7 %collective-permute-start.28 = (bf16[208,512]{1,0:T(8,128)(2,1)S(1)}, bf16[208,512]{1,0:T(8,128)(2,1)S(1)}, u32[]{:S(2)}, u32[]{:S(2)}) collective-permute-start(bf16[208,512]{1,0:T(8,128)(2,1)S(1)} %copy-done.47), channel_id=1, source_target_pairs={{0,24},{4,28},{8,16},{12,20},{16,8},{20,12},{24,0},{28,4},{1,25},{... | collective-permute-start | bytes 638984 | tf_op jit(solution)/shard_map/ppermute | solution.py:536
  212.5 5.8 %collective-permute-done.24.refs_2_ = bf16[208,512]{1,0:T(8,128)(2,1)S(1)} collective-permute-done((bf16[208,512]{1,0:T(8,128)(2,1)S(1)}, bf16[208,512]{1,0:T(8,128)(2,1)S(1)}, u32[]{:S(2)}, u32[]{:S(2)}) %collective-permute-start.24) | collective-permute-done | bytes 213024 | tf_op jit(solution)/shard_map/ppermute | solution.py:536
  218.3 3.8 %collective-permute-start.29 = (bf16[208,512]{1,0:T(8,128)(2,1)S(1)}, bf16[208,512]{1,0:T(8,128)(2,1)S(1)}, u32[]{:S(2)}, u32[]{:S(2)}) collective-permute-start(bf16[208,512]{1,0:T(8,128)(2,1)S(1)} %copy-done.46), channel_id=1, source_target_pairs={{0,28},{4,24},{8,20},{12,16},{16,12},{20,8},{24,4},{28,0},{1,29},{... | collective-permute-start | bytes 638984 | tf_op jit(solution)/shard_map/ppermute | solution.py:536
  222.9 24.5 %collective-permute-done.26.refs_4_ = bf16[208,512]{1,0:T(8,128)(2,1)S(1)} collective-permute-done((bf16[208,512]{1,0:T(8,128)(2,1)S(1)}, bf16[208,512]{1,0:T(8,128)(2,1)S(1)}, u32[]{:S(2)}, u32[]{:S(2)}) %collective-permute-start.26) | collective-permute-done | bytes 213024 | tf_op jit(solution)/shard_map/ppermute | solution.py:536
  247.4 5.3 %collective-permute-done.27.refs_5_ = bf16[208,512]{1,0:T(8,128)(2,1)S(1)} collective-permute-done((bf16[208,512]{1,0:T(8,128)(2,1)S(1)}, bf16[208,512]{1,0:T(8,128)(2,1)S(1)}, u32[]{:S(2)}, u32[]{:S(2)}) %collective-permute-start.27) | collective-permute-done | bytes 213024 | tf_op jit(solution)/shard_map/ppermute | solution.py:536
  253.5 9.3 %shard_map.225 = (f32[512,512]{1,0:T(8,128)}, bf16[512,512]{1,0:T(8,128)(2,1)}, f32[256,768]{1,0:T(8,128)}, bf16[256,768]{1,0:T(8,128)(2,1)}) custom-call(s32[1]{0:T(128)} %bitcast.me_ref, f32[512,128]{1,0:T(8,128)} %get-tuple-element.70.side_ref, f32[512,512]{1,0:T(8,128)} %get-tuple-element.72.hidden_ref, f32[512,128]{1,0:T(8,128)} %get-tuple-element.73.gates_ref, ...), custom_call_target="tpu_custom_call" | custom-call | flops 1879048192 | bytes 9437188 | tf_op jit(solution)/shard_map/pallas_call | solution.py:75
  262.8 18.3 %shard_map.226 = (f32[512,512]{1,0:T(8,128)}, f32[256,1664]{1,0:T(8,128)}, bf16[256,1664]{1,0:T(8,128)(2,1)}) custom-call(s32[1]{0:T(128)} %bitcast.me_ref, f32[512,128]{1,0:T(8,128)} %get-tuple-element.70.side_ref, f32[8,512]{1,0:T(8,128)} %get-tuple-element.71.rows_ref, bf16[512,512]{1,0:T(8,128)(2,1)} %tokens_ref.3, ...), custom_call_target="tpu_custom_call" | custom-call | flops 3221225472 | bytes 10174468 | tf_op jit(solution)/shard_map/pallas_call | solution.py:75
  282.9 2.1 shard_map.230
  287.2 2.8 collective-permute-done.38.refs_0_
  290.0 1.6 collective-permute-start.40
  291.7 4.0 %collective-permute-done.40.refs_2_ = bf16[64,768]{1,0:T(8,128)(2,1)S(1)} collective-permute-done((bf16[64,768]{1,0:T(8,128)(2,1)}, bf16[64,768]{1,0:T(8,128)(2,1)S(1)}, u32[]{:S(2)}, u32[]{:S(2)}) %collective-permute-start.40) | collective-permute-done | bytes 98336 | tf_op jit(solution)/shard_map/ppermute | solution.py:144
  296.4 1.7 shard_map.231
  298.1 8.5 %collective-permute-start.41 = (bf16[16,768]{1,0:T(8,128)(2,1)}, bf16[16,768]{1,0:T(8,128)(2,1)S(1)}, u32[]{:S(2)}, u32[]{:S(2)}) collective-permute-start(bf16[16,768]{1,0:T(8,128)(2,1)} %get-tuple-element.116), channel_id=1, source_target_pairs={{0,8},{1,9},{2,10},{3,11},{4,12},{5,13},{6,14},{7,15},{8,0},{9,1},... | collective-permute-start | bytes 73736 | tf_op jit(solution)/shard_map/ppermute | solution.py:144
  307.8 2.7 shard_map.227
  310.5 2.3 collective-permute-start.43
  317.7 3.6 collective-permute-done.31.refs_0_
  324.7 4.9 %collective-permute-done.33.refs_2_ = bf16[64,1664]{1,0:T(8,128)(2,1)S(1)} collective-permute-done((bf16[64,1664]{1,0:T(8,128)(2,1)S(1)}, bf16[64,1664]{1,0:T(8,128)(2,1)S(1)}, u32[]{:S(2)}, u32[]{:S(2)}) %collective-permute-start.33) | collective-permute-done | bytes 213024 | tf_op jit(solution)/shard_map/ppermute | solution.py:144
  330.3 1.9 shard_map.228
  334.3 2.4 collective-permute-start.36
  336.7 1.5 slice_reduce_fusion
  340.8 5.9 %collective-permute-done.49.more_out = bf16[512,512]{1,0:T(8,128)(2,1)S(1)} collective-permute-done((bf16[512,512]{1,0:T(8,128)(2,1)S(1)}, bf16[512,512]{1,0:T(8,128)(2,1)S(1)}, u32[]{:S(2)}, u32[]{:S(2)}) %collective-permute-start.49) | collective-permute-done | bytes 524320 | tf_op jit(solution)/shard_map/ppermute | solution.py:531
  347.5 3.8 %shard_map.233 = (f32[512,512]{1,0:T(8,128)}, f32[512,512]{1,0:T(8,128)}) custom-call(f32[512,512]{1,0:T(8,128)} %get-tuple-element.119.own_in, f32[512,512]{1,0:T(8,128)} %get-tuple-element.120.own_out, bf16[512,512]{1,0:T(8,128)(2,1)} %copy-done.5, bf16[512,512]{1,0:T(8,128)(2,1)} %copy-done.6, bf16[512,512]{1,0:T(8,128)(2,1)} %copy-done.7, ...), custom_call_target="tpu_custom_call" | custom-call | flops 1048576 | bytes 6291456 | tf_op jit(solution)/shard_map/pallas_call | solution.py:75
  352.0 1.6 shard_map.229
  353.6 1.5 slice.28
  357.8 5.1 %shard_map.224 = bf16[512,512]{1,0:T(8,128)(2,1)} custom-call(f32[512,128]{1,0:T(8,128)} %get-tuple-element.70.side_ref, f32[512,512]{1,0:T(8,128)} %get-tuple-element.72.hidden_ref, f32[512,128]{1,0:T(8,128)} %get-tuple-element.73.gates_ref, bf16[8,192,512]{2,1,0:T(8,128)(2,1)} %copy-done), custom_call_target="tpu_custom_call" | custom-call | flops 1610612736 | bytes 3670016 | tf_op jit(solution)/shard_map/pallas_call | solution.py:75
  (216 shorter events, 39.7 us)
Async XLA Ops:
  7.1 130.4 %all-to-all-start = ((bf16[8,192,512]{2,1,0:T(8,128)(2,1)}), bf16[8,192,512]{2,1,0:T(8,128)(2,1)S(1)}, u32[]{:S(2)}, u32[]{:S(2)}) async-start(bf16[8,192,512]{2,1,0:T(8,128)(2,1)} %get-tuple-element.74), calls=%async_computation | async-start | bytes 3145728 | tf_op jit(solution)/shard_map/all_to_all | solution.py:623
  15.0 32.1 %collective-permute-start.2 = (bf16[16,2304]{1,0:T(8,128)(2,1)S(1)}, bf16[16,2304]{1,0:T(8,128)(2,1)S(1)}, u32[]{:S(2)}, u32[]{:S(2)}) collective-permute-start(bf16[16,2304]{1,0:T(8,128)(2,1)S(1)} %concatenate.6), channel_id=1, source_target_pairs={{0,24},{1,25},{2,26},{3,27},{4,28},{5,29},{6,30},{7,31},{8,16},{9,... | collective-permute-start | bytes 221192 | tf_op jit(solution)/shard_map/ppermute | solution.py:144
  18.8 39.0 %collective-permute-start.1 = (bf16[16,2304]{1,0:T(8,128)(2,1)S(1)}, bf16[16,2304]{1,0:T(8,128)(2,1)S(1)}, u32[]{:S(2)}, u32[]{:S(2)}) collective-permute-start(bf16[16,2304]{1,0:T(8,128)(2,1)S(1)} %concatenate.6), channel_id=1, source_target_pairs={{0,16},{1,17},{2,18},{3,19},{4,20},{5,21},{6,22},{7,23},{8,24},{9,... | collective-permute-start | bytes 221192 | tf_op jit(solution)/shard_map/ppermute | solution.py:144
  18.8 39.0 %collective-permute-start = (bf16[16,2304]{1,0:T(8,128)(2,1)S(1)}, bf16[16,2304]{1,0:T(8,128)(2,1)S(1)}, u32[]{:S(2)}, u32[]{:S(2)}) collective-permute-start(bf16[16,2304]{1,0:T(8,128)(2,1)S(1)} %concatenate.6), channel_id=1, source_target_pairs={{0,8},{1,9},{2,10},{3,11},{4,12},{5,13},{6,14},{7,15},{8,0},{9,1},... | collective-permute-start | bytes 221192 | tf_op jit(solution)/shard_map/ppermute | solution.py:144
  57.9 11.0 %collective-permute-start.5 = (bf16[64,2304]{1,0:T(8,128)(2,1)S(1)}, bf16[64,2304]{1,0:T(8,128)(2,1)S(1)}, u32[]{:S(2)}, u32[]{:S(2)}) collective-permute-start(bf16[64,2304]{1,0:T(8,128)(2,1)S(1)} %pad_maximum_fusion.refs_0_), channel_id=1, source_target_pairs={{0,6},{1,7},{2,4},{3,5},{4,2},{5,3},{6,0},{7,1},{8,14},{9,15},{10,... | collective-permute-start | bytes 884744 | tf_op jit(solution)/shard_map/ppermute | solution.py:144
  60.3 12.3 %collective-permute-start.4 = (bf16[64,2304]{1,0:T(8,128)(2,1)S(1)}, bf16[64,2304]{1,0:T(8,128)(2,1)S(1)}, u32[]{:S(2)}, u32[]{:S(2)}) collective-permute-start(bf16[64,2304]{1,0:T(8,128)(2,1)S(1)} %pad_maximum_fusion.refs_0_), channel_id=1, source_target_pairs={{0,4},{1,5},{2,6},{3,7},{4,0},{5,1},{6,2},{7,3},{8,12},{9,13},{10,... | collective-permute-start | bytes 884744 | tf_op jit(solution)/shard_map/ppermute | solution.py:144
  60.9 11.8 %collective-permute-start.3 = (bf16[64,2304]{1,0:T(8,128)(2,1)S(1)}, bf16[64,2304]{1,0:T(8,128)(2,1)}, u32[]{:S(2)}, u32[]{:S(2)}) collective-permute-start(bf16[64,2304]{1,0:T(8,128)(2,1)S(1)} %pad_maximum_fusion.refs_0_), channel_id=1, source_target_pairs={{0,2},{1,3},{2,0},{3,1},{4,6},{5,7},{6,4},{7,5},{8,10},{9,11},{10,... | collective-permute-start | bytes 884744 | tf_op jit(solution)/shard_map/ppermute | solution.py:144
  61.4 12.7 %collective-permute-start.6 = (bf16[64,2304]{1,0:T(8,128)(2,1)S(1)}, bf16[64,2304]{1,0:T(8,128)(2,1)S(1)}, u32[]{:S(2)}, u32[]{:S(2)}) collective-permute-start(bf16[64,2304]{1,0:T(8,128)(2,1)S(1)} %pad_maximum_fusion.refs_0_), channel_id=1, source_target_pairs={{0,1},{1,0},{2,3},{3,2},{4,5},{5,4},{6,7},{7,6},{8,9},{9,8},{10,11... | collective-permute-start | bytes 884744 | tf_op jit(solution)/shard_map/ppermute | solution.py:144
  68.8 6.4 %collective-permute-start.9 = (bf16[64,2304]{1,0:T(8,128)(2,1)S(1)}, bf16[64,2304]{1,0:T(8,128)(2,1)S(1)}, u32[]{:S(2)}, u32[]{:S(2)}) collective-permute-start(bf16[64,2304]{1,0:T(8,128)(2,1)S(1)} %collective-permute-done.5.refs_3_), channel_id=1, source_target_pairs={{0,1},{1,0},{2,3},{3,2},{4,5},{5,4},{6,7},{7,6},{8,9},{9,8},{10,11... | collective-permute-start | bytes 884744 | tf_op jit(solution)/shard_map/ppermute | solution.py:144
  73.1 20.6 %collective-permute-start.18 = (bf16[512,512]{1,0:T(8,128)(2,1)S(1)}, bf16[512,512]{1,0:T(8,128)(2,1)S(1)}, u32[]{:S(2)}, u32[]{:S(2)}) collective-permute-start(bf16[512,512]{1,0:T(8,128)(2,1)S(1)} %bitcast.16), channel_id=1, source_target_pairs={{0,2},{1,3},{2,0},{3,1},{4,6},{5,7},{6,4},{7,5},{8,10},{9,11},{10,... | collective-permute-start | bytes 1572872 | tf_op jit(solution)/shard_map/ppermute | solution.py:531
  74.1 24.2 %collective-permute-start.21 = (bf16[512,512]{1,0:T(8,128)(2,1)S(1)}, bf16[512,512]{1,0:T(8,128)(2,1)}, u32[]{:S(2)}, u32[]{:S(2)}) collective-permute-start(bf16[512,512]{1,0:T(8,128)(2,1)S(1)} %bitcast.19), channel_id=1, source_target_pairs={{0,2},{1,3},{2,0},{3,1},{4,6},{5,7},{6,4},{7,5},{8,10},{9,11},{10,... | collective-permute-start | bytes 1572872 | tf_op jit(solution)/shard_map/ppermute | solution.py:531
  75.2 23.2 %collective-permute-start.17 = (bf16[512,512]{1,0:T(8,128)(2,1)S(1)}, bf16[512,512]{1,0:T(8,128)(2,1)}, u32[]{:S(2)}, u32[]{:S(2)}) collective-permute-start(bf16[512,512]{1,0:T(8,128)(2,1)S(1)} %bitcast.17), channel_id=1, source_target_pairs={{0,1},{1,0},{2,3},{3,2},{4,5},{5,4},{6,7},{7,6},{8,9},{9,8},{10,11... | collective-permute-start | bytes 1572872 | tf_op jit(solution)/shard_map/ppermute | solution.py:531
  75.2 23.9 %collective-permute-start.20 = (bf16[512,512]{1,0:T(8,128)(2,1)S(1)}, bf16[512,512]{1,0:T(8,128)(2,1)}, u32[]{:S(2)}, u32[]{:S(2)}) collective-permute-start(bf16[512,512]{1,0:T(8,128)(2,1)S(1)} %bitcast.20), channel_id=1, source_target_pairs={{0,1},{1,0},{2,3},{3,2},{4,5},{5,4},{6,7},{7,6},{8,9},{9,8},{10,11... | collective-permute-start | bytes 1572872 | tf_op jit(solution)/shard_map/ppermute | solution.py:531
  91.9 9.7 %collective-permute-start.10 = (bf16[208,512]{1,0:T(8,128)(2,1)}, bf16[208,512]{1,0:T(8,128)(2,1)S(1)}, u32[]{:S(2)}, u32[]{:S(2)}) collective-permute-start(bf16[208,512]{1,0:T(8,128)(2,1)} %get-tuple-element.76), channel_id=1, source_target_pairs={{0,4},{4,0},{8,12},{12,8},{16,20},{20,16},{24,28},{28,24},{1,5},{5... | collective-permute-start | bytes 638984 | tf_op jit(solution)/shard_map/ppermute | solution.py:536
  93.7 42.2 %collective-permute-start.19 = (bf16[512,512]{1,0:T(8,128)(2,1)S(1)}, bf16[512,512]{1,0:T(8,128)(2,1)S(1)}, u32[]{:S(2)}, u32[]{:S(2)}) collective-permute-start(bf16[512,512]{1,0:T(8,128)(2,1)S(1)} %collective-permute-done.18.refs_10_), channel_id=1, source_target_pairs={{0,1},{1,0},{2,3},{3,2},{4,5},{5,4},{6,7},{7,6},{8,9},{9,8},{10,11... | collective-permute-start | bytes 1572872 | tf_op jit(solution)/shard_map/ppermute | solution.py:531
  98.3 39.1 %collective-permute-start.22 = (bf16[512,512]{1,0:T(8,128)(2,1)}, bf16[512,512]{1,0:T(8,128)(2,1)}, u32[]{:S(2)}, u32[]{:S(2)}) collective-permute-start(bf16[512,512]{1,0:T(8,128)(2,1)} %collective-permute-done.21.refs_14_), channel_id=1, source_target_pairs={{0,1},{1,0},{2,3},{3,2},{4,5},{5,4},{6,7},{7,6},{8,9},{9,8},{10,11... | collective-permute-start | bytes 1572872 | tf_op jit(solution)/shard_map/ppermute | solution.py:531
  98.4 12.8 %collective-permute-start.11 = (bf16[208,512]{1,0:T(8,128)(2,1)}, bf16[208,512]{1,0:T(8,128)(2,1)S(1)}, u32[]{:S(2)}, u32[]{:S(2)}) collective-permute-start(bf16[208,512]{1,0:T(8,128)(2,1)} %get-tuple-element.77), channel_id=1, source_target_pairs={{0,8},{4,12},{8,0},{12,4},{16,24},{20,28},{24,16},{28,20},{1,9},{5... | collective-permute-start | bytes 638984 | tf_op jit(solution)/shard_map/ppermute | solution.py:536
  99.1 17.5 %collective-permute-start.12 = (bf16[208,512]{1,0:T(8,128)(2,1)}, bf16[208,512]{1,0:T(8,128)(2,1)S(1)}, u32[]{:S(2)}, u32[]{:S(2)}) collective-permute-start(bf16[208,512]{1,0:T(8,128)(2,1)} %get-tuple-element.78), channel_id=1, source_target_pairs={{0,12},{4,8},{8,4},{12,0},{16,28},{20,24},{24,20},{28,16},{1,13},{... | collective-permute-start | bytes 638984 | tf_op jit(solution)/shard_map/ppermute | solution.py:536
  101.6 17.8 %collective-permute-start.13 = (bf16[208,512]{1,0:T(8,128)(2,1)}, bf16[208,512]{1,0:T(8,128)(2,1)S(1)}, u32[]{:S(2)}, u32[]{:S(2)}) collective-permute-start(bf16[208,512]{1,0:T(8,128)(2,1)} %get-tuple-element.79), channel_id=1, source_target_pairs={{0,16},{4,20},{8,24},{12,28},{16,0},{20,4},{24,8},{28,12},{1,17},{... | collective-permute-start | bytes 638984 | tf_op jit(solution)/shard_map/ppermute | solution.py:536
  111.2 24.7 %collective-permute-start.14 = (bf16[208,512]{1,0:T(8,128)(2,1)}, bf16[208,512]{1,0:T(8,128)(2,1)S(1)}, u32[]{:S(2)}, u32[]{:S(2)}) collective-permute-start(bf16[208,512]{1,0:T(8,128)(2,1)} %get-tuple-element.80), channel_id=1, source_target_pairs={{0,20},{4,16},{8,28},{12,24},{16,4},{20,0},{24,12},{28,8},{1,21},{... | collective-permute-start | bytes 638984 | tf_op jit(solution)/shard_map/ppermute | solution.py:536
  116.6 19.3 %collective-permute-start.15 = (bf16[208,512]{1,0:T(8,128)(2,1)}, bf16[208,512]{1,0:T(8,128)(2,1)S(1)}, u32[]{:S(2)}, u32[]{:S(2)}) collective-permute-start(bf16[208,512]{1,0:T(8,128)(2,1)} %get-tuple-element.81), channel_id=1, source_target_pairs={{0,24},{4,28},{8,16},{12,20},{16,8},{20,12},{24,0},{28,4},{1,25},{... | collective-permute-start | bytes 638984 | tf_op jit(solution)/shard_map/ppermute | solution.py:536
  119.4 16.6 %collective-permute-start.16 = (bf16[208,512]{1,0:T(8,128)(2,1)}, bf16[208,512]{1,0:T(8,128)(2,1)S(1)}, u32[]{:S(2)}, u32[]{:S(2)}) collective-permute-start(bf16[208,512]{1,0:T(8,128)(2,1)} %get-tuple-element.82), channel_id=1, source_target_pairs={{0,28},{4,24},{8,20},{12,16},{16,12},{20,8},{24,4},{28,0},{1,29},{... | collective-permute-start | bytes 638984 | tf_op jit(solution)/shard_map/ppermute | solution.py:536
  174.6 182.0 %all-to-all-start.1 = ((bf16[8,192,512]{2,1,0:T(8,128)(2,1)}), bf16[8,192,512]{2,1,0:T(8,128)(2,1)S(1)}, u32[]{:S(2)}, u32[]{:S(2)}) async-start(bf16[8,192,512]{2,1,0:T(8,128)(2,1)} %get-tuple-element.83), calls=%async_computation.1 | async-start | bytes 3145728 | tf_op jit(solution)/shard_map/all_to_all | solution.py:671
  186.2 18.7 %collective-permute-start.23 = (bf16[208,512]{1,0:T(8,128)(2,1)S(1)}, bf16[208,512]{1,0:T(8,128)(2,1)S(1)}, u32[]{:S(2)}, u32[]{:S(2)}) collective-permute-start(bf16[208,512]{1,0:T(8,128)(2,1)S(1)} %copy-done.57), channel_id=1, source_target_pairs={{0,4},{4,0},{8,12},{12,8},{16,20},{20,16},{24,28},{28,24},{1,5},{5... | collective-permute-start | bytes 638984 | tf_op jit(solution)/shard_map/ppermute | solution.py:536
  188.2 30.2 %collective-permute-start.24 = (bf16[208,512]{1,0:T(8,128)(2,1)S(1)}, bf16[208,512]{1,0:T(8,128)(2,1)S(1)}, u32[]{:S(2)}, u32[]{:S(2)}) collective-permute-start(bf16[208,512]{1,0:T(8,128)(2,1)S(1)} %copy-done.53), channel_id=1, source_target_pairs={{0,8},{4,12},{8,0},{12,4},{16,24},{20,28},{24,16},{28,20},{1,9},{5... | collective-permute-start | bytes 638984 | tf_op jit(solution)/shard_map/ppermute | solution.py:536
  189.6 33.3 %collective-permute-start.25 = (bf16[208,512]{1,0:T(8,128)(2,1)S(1)}, bf16[208,512]{1,0:T(8,128)(2,1)S(1)}, u32[]{:S(2)}, u32[]{:S(2)}) collective-permute-start(bf16[208,512]{1,0:T(8,128)(2,1)S(1)} %copy-done.51), channel_id=1, source_target_pairs={{0,12},{4,8},{8,4},{12,0},{16,28},{20,24},{24,20},{28,16},{1,13},{... | collective-permute-start | bytes 638984 | tf_op jit(solution)/shard_map/ppermute | solution.py:536
  189.7 57.6 %collective-permute-start.26 = (bf16[208,512]{1,0:T(8,128)(2,1)S(1)}, bf16[208,512]{1,0:T(8,128)(2,1)S(1)}, u32[]{:S(2)}, u32[]{:S(2)}) collective-permute-start(bf16[208,512]{1,0:T(8,128)(2,1)S(1)} %copy-done.50), channel_id=1, source_target_pairs={{0,16},{4,20},{8,24},{12,28},{16,0},{20,4},{24,8},{28,12},{1,17},{... | collective-permute-start | bytes 638984 | tf_op jit(solution)/shard_map/ppermute | solution.py:536
  192.6 60.1 %collective-permute-start.27 = (bf16[208,512]{1,0:T(8,128)(2,1)S(1)}, bf16[208,512]{1,0:T(8,128)(2,1)S(1)}, u32[]{:S(2)}, u32[]{:S(2)}) collective-permute-start(bf16[208,512]{1,0:T(8,128)(2,1)S(1)} %copy-done.48), channel_id=1, source_target_pairs={{0,20},{4,16},{8,28},{12,24},{16,4},{20,0},{24,12},{28,8},{1,21},{... | collective-permute-start | bytes 638984 | tf_op jit(solution)/shard_map/ppermute | solution.py:536
  204.8 47.8 %collective-permute-start.28 = (bf16[208,512]{1,0:T(8,128)(2,1)S(1)}, bf16[208,512]{1,0:T(8,128)(2,1)S(1)}, u32[]{:S(2)}, u32[]{:S(2)}) collective-permute-start(bf16[208,512]{1,0:T(8,128)(2,1)S(1)} %copy-done.47), channel_id=1, source_target_pairs={{0,24},{4,28},{8,16},{12,20},{16,8},{20,12},{24,0},{28,4},{1,25},{... | collective-permute-start | bytes 638984 | tf_op jit(solution)/shard_map/ppermute | solution.py:536
  218.3 34.3 %collective-permute-start.29 = (bf16[208,512]{1,0:T(8,128)(2,1)S(1)}, bf16[208,512]{1,0:T(8,128)(2,1)S(1)}, u32[]{:S(2)}, u32[]{:S(2)}) collective-permute-start(bf16[208,512]{1,0:T(8,128)(2,1)S(1)} %copy-done.46), channel_id=1, source_target_pairs={{0,28},{4,24},{8,20},{12,16},{16,12},{20,8},{24,4},{28,0},{1,29},{... | collective-permute-start | bytes 638984 | tf_op jit(solution)/shard_map/ppermute | solution.py:536
  262.8 19.4 %collective-permute-start.37 = (bf16[256,768]{1,0:T(8,128)(2,1)}, bf16[256,768]{1,0:T(8,128)(2,1)S(1)}, u32[]{:S(2)}, u32[]{:S(2)}) collective-permute-start(bf16[256,768]{1,0:T(8,128)(2,1)} %get-tuple-element.110), channel_id=1, source_target_pairs={{0,1},{1,0},{2,3},{3,2},{4,5},{5,4},{6,7},{7,6},{8,9},{9,8},{10,11... | collective-permute-start | bytes 1179656 | tf_op jit(solution)/shard_map/ppermute | solution.py:144
  281.2 25.7 %collective-permute-start.30 = (bf16[256,1664]{1,0:T(8,128)(2,1)}, bf16[256,1664]{1,0:T(8,128)(2,1)S(1)}, u32[]{:S(2)}, u32[]{:S(2)}) collective-permute-start(bf16[256,1664]{1,0:T(8,128)(2,1)} %get-tuple-element.100), channel_id=1, source_target_pairs={{0,1},{1,0},{2,3},{3,2},{4,5},{5,4},{6,7},{7,6},{8,9},{9,8},{10,11... | collective-permute-start | bytes 2555912 | tf_op jit(solution)/shard_map/ppermute | solution.py:144
  281.7 24.9 %collective-permute-start.46 = (bf16[512,512]{1,0:T(8,128)(2,1)S(1)}, bf16[512,512]{1,0:T(8,128)(2,1)S(1)}, u32[]{:S(2)}, u32[]{:S(2)}) collective-permute-start(bf16[512,512]{1,0:T(8,128)(2,1)S(1)} %copy-done.35), channel_id=1, source_target_pairs={{0,1},{1,0},{2,3},{3,2},{4,5},{5,4},{6,7},{7,6},{8,9},{9,8},{10,11... | collective-permute-start | bytes 1572872 | tf_op jit(solution)/shard_map/ppermute | solution.py:531
  281.8 28.8 %collective-permute-start.48 = (bf16[512,512]{1,0:T(8,128)(2,1)S(1)}, bf16[512,512]{1,0:T(8,128)(2,1)S(1)}, u32[]{:S(2)}, u32[]{:S(2)}) collective-permute-start(bf16[512,512]{1,0:T(8,128)(2,1)S(1)} %copy-done.34), channel_id=1, source_target_pairs={{0,1},{1,0},{2,3},{3,2},{4,5},{5,4},{6,7},{7,6},{8,9},{9,8},{10,11... | collective-permute-start | bytes 1572872 | tf_op jit(solution)/shard_map/ppermute | solution.py:531
  290.0 5.7 %collective-permute-start.40 = (bf16[64,768]{1,0:T(8,128)(2,1)}, bf16[64,768]{1,0:T(8,128)(2,1)S(1)}, u32[]{:S(2)}, u32[]{:S(2)}) collective-permute-start(bf16[64,768]{1,0:T(8,128)(2,1)} %get-tuple-element.114), channel_id=1, source_target_pairs={{0,6},{1,7},{2,4},{3,5},{4,2},{5,3},{6,0},{7,1},{8,14},{9,15},{10,... | collective-permute-start | bytes 294920 | tf_op jit(solution)/shard_map/ppermute | solution.py:144
  291.7 41.6 %collective-permute-start.44 = (bf16[512,512]{1,0:T(8,128)(2,1)S(1)}, bf16[512,512]{1,0:T(8,128)(2,1)S(1)}, u32[]{:S(2)}, u32[]{:S(2)}) collective-permute-start(bf16[512,512]{1,0:T(8,128)(2,1)S(1)} %copy-done.33), channel_id=1, source_target_pairs={{0,1},{1,0},{2,3},{3,2},{4,5},{5,4},{6,7},{7,6},{8,9},{9,8},{10,11... | collective-permute-start | bytes 1572872 | tf_op jit(solution)/shard_map/ppermute | solution.py:531
  298.1 14.7 %collective-permute-start.41 = (bf16[16,768]{1,0:T(8,128)(2,1)}, bf16[16,768]{1,0:T(8,128)(2,1)S(1)}, u32[]{:S(2)}, u32[]{:S(2)}) collective-permute-start(bf16[16,768]{1,0:T(8,128)(2,1)} %get-tuple-element.116), channel_id=1, source_target_pairs={{0,8},{1,9},{2,10},{3,11},{4,12},{5,13},{6,14},{7,15},{8,0},{9,1},... | collective-permute-start | bytes 73736 | tf_op jit(solution)/shard_map/ppermute | solution.py:144
  306.6 7.7 %collective-permute-start.42 = (bf16[16,768]{1,0:T(8,128)(2,1)}, bf16[16,768]{1,0:T(8,128)(2,1)S(1)}, u32[]{:S(2)}, u32[]{:S(2)}) collective-permute-start(bf16[16,768]{1,0:T(8,128)(2,1)} %get-tuple-element.117), channel_id=1, source_target_pairs={{0,16},{1,17},{2,18},{3,19},{4,20},{5,21},{6,22},{7,23},{8,24},{9,... | collective-permute-start | bytes 73736 | tf_op jit(solution)/shard_map/ppermute | solution.py:144
  307.0 27.3 %collective-permute-start.45 = (bf16[512,512]{1,0:T(8,128)(2,1)S(1)}, bf16[512,512]{1,0:T(8,128)(2,1)S(1)}, u32[]{:S(2)}, u32[]{:S(2)}) collective-permute-start(bf16[512,512]{1,0:T(8,128)(2,1)S(1)} %copy-done.32), channel_id=1, source_target_pairs={{0,1},{1,0},{2,3},{3,2},{4,5},{5,4},{6,7},{7,6},{8,9},{9,8},{10,11... | collective-permute-start | bytes 1572872 | tf_op jit(solution)/shard_map/ppermute | solution.py:531
  310.5 5.7 %collective-permute-start.43 = (bf16[16,768]{1,0:T(8,128)(2,1)S(1)}, bf16[16,768]{1,0:T(8,128)(2,1)S(1)}, u32[]{:S(2)}, u32[]{:S(2)}) collective-permute-start(bf16[16,768]{1,0:T(8,128)(2,1)S(1)} %copy-done.65), channel_id=1, source_target_pairs={{0,24},{1,25},{2,26},{3,27},{4,28},{5,29},{6,30},{7,31},{8,16},{9,... | collective-permute-start | bytes 73736 | tf_op jit(solution)/shard_map/ppermute | solution.py:144
  312.9 8.4 %collective-permute-start.31 = (bf16[64,1664]{1,0:T(8,128)(2,1)}, bf16[64,1664]{1,0:T(8,128)(2,1)S(1)}, u32[]{:S(2)}, u32[]{:S(2)}) collective-permute-start(bf16[64,1664]{1,0:T(8,128)(2,1)} %get-tuple-element.102), channel_id=1, source_target_pairs={{0,2},{1,3},{2,0},{3,1},{4,6},{5,7},{6,4},{7,5},{8,10},{9,11},{10,... | collective-permute-start | bytes 638984 | tf_op jit(solution)/shard_map/ppermute | solution.py:144
  314.3 8.4 %collective-permute-start.32 = (bf16[64,1664]{1,0:T(8,128)(2,1)}, bf16[64,1664]{1,0:T(8,128)(2,1)S(1)}, u32[]{:S(2)}, u32[]{:S(2)}) collective-permute-start(bf16[64,1664]{1,0:T(8,128)(2,1)} %get-tuple-element.103), channel_id=1, source_target_pairs={{0,4},{1,5},{2,6},{3,7},{4,0},{5,1},{6,2},{7,3},{8,12},{9,13},{10,... | collective-permute-start | bytes 638984 | tf_op jit(solution)/shard_map/ppermute | solution.py:144
  316.2 24.6 %collective-permute-start.47 = (bf16[512,512]{1,0:T(8,128)(2,1)S(1)}, bf16[512,512]{1,0:T(8,128)(2,1)S(1)}, u32[]{:S(2)}, u32[]{:S(2)}) collective-permute-start(bf16[512,512]{1,0:T(8,128)(2,1)S(1)} %add_convert_fusion.1), channel_id=1, source_target_pairs={{0,2},{1,3},{2,0},{3,1},{4,6},{5,7},{6,4},{7,5},{8,10},{9,11},{10,... | collective-permute-start | bytes 1572872 | tf_op jit(solution)/shard_map/ppermute | solution.py:531
  321.3 25.4 %collective-permute-start.49 = (bf16[512,512]{1,0:T(8,128)(2,1)S(1)}, bf16[512,512]{1,0:T(8,128)(2,1)S(1)}, u32[]{:S(2)}, u32[]{:S(2)}) collective-permute-start(bf16[512,512]{1,0:T(8,128)(2,1)S(1)} %add_convert_fusion), channel_id=1, source_target_pairs={{0,2},{1,3},{2,0},{3,1},{4,6},{5,7},{6,4},{7,5},{8,10},{9,11},{10,... | collective-permute-start | bytes 1572872 | tf_op jit(solution)/shard_map/ppermute | solution.py:531
  322.7 6.9 %collective-permute-start.33 = (bf16[64,1664]{1,0:T(8,128)(2,1)S(1)}, bf16[64,1664]{1,0:T(8,128)(2,1)S(1)}, u32[]{:S(2)}, u32[]{:S(2)}) collective-permute-start(bf16[64,1664]{1,0:T(8,128)(2,1)S(1)} %copy-done.55), channel_id=1, source_target_pairs={{0,6},{1,7},{2,4},{3,5},{4,2},{5,3},{6,0},{7,1},{8,14},{9,15},{10,... | collective-permute-start | bytes 638984 | tf_op jit(solution)/shard_map/ppermute | solution.py:144
  332.3 19.1 %collective-permute-start.34 = (bf16[16,1664]{1,0:T(8,128)(2,1)}, bf16[16,1664]{1,0:T(8,128)(2,1)S(1)}, u32[]{:S(2)}, u32[]{:S(2)}) collective-permute-start(bf16[16,1664]{1,0:T(8,128)(2,1)} %get-tuple-element.106), channel_id=1, source_target_pairs={{0,8},{1,9},{2,10},{3,11},{4,12},{5,13},{6,14},{7,15},{8,0},{9,1},... | collective-permute-start | bytes 159752 | tf_op jit(solution)/shard_map/ppermute | solution.py:144
  333.3 18.0 %collective-permute-start.35 = (bf16[16,1664]{1,0:T(8,128)(2,1)}, bf16[16,1664]{1,0:T(8,128)(2,1)S(1)}, u32[]{:S(2)}, u32[]{:S(2)}) collective-permute-start(bf16[16,1664]{1,0:T(8,128)(2,1)} %get-tuple-element.107), channel_id=1, source_target_pairs={{0,16},{1,17},{2,18},{3,19},{4,20},{5,21},{6,22},{7,23},{8,24},{9,... | collective-permute-start | bytes 159752 | tf_op jit(solution)/shard_map/ppermute | solution.py:144
  334.3 17.1 %collective-permute-start.36 = (bf16[16,1664]{1,0:T(8,128)(2,1)}, bf16[16,1664]{1,0:T(8,128)(2,1)S(1)}, u32[]{:S(2)}, u32[]{:S(2)}) collective-permute-start(bf16[16,1664]{1,0:T(8,128)(2,1)} %get-tuple-element.108), channel_id=1, source_target_pairs={{0,24},{1,25},{2,26},{3,27},{4,28},{5,29},{6,30},{7,31},{8,16},{9,... | collective-permute-start | bytes 159752 | tf_op jit(solution)/shard_map/ppermute | solution.py:144
  (70 other events, 882.3 us)
